TPU v7x, 1024 devices: a whole 4x8x16 slice. The times are simulated.
1024 devices in a mesh: dp: 8 (over y), expert: 16 (over z), tensor: 8 (over x, core).
Axes of the slice: x: 4, y: 8, z: 16, core: 2. Of those that a mesh axis runs over, the one named last changes fastest.
Arguments:
- activations: bfloat16 [16384, 4096], P(('dp', 'expert'), 'tensor'), parts along dimension 0, may hold values from -6 to 6
- expert_ids: int32 [16384, 8], P(('dp', 'expert')), parts along dimension 0, may hold values from 0 to 31, all different within a row; in each aligned block of 128 rows (0 to 127, 128 to 255, ...) at most 48 rows name the same one
- route_gates: float32 [16384, 8], P(('dp', 'expert')), parts along dimension 0, may hold values from 0.1 to 1
- down_proj: bfloat16 [4096, 1024], P('tensor'), may hold values from -0.09375 to 0.09375
- expert_gate: bfloat16 [32, 1024, 2688], P('expert', None, 'tensor'), may hold values from -0.1875 to 0.1875
- expert_up: bfloat16 [32, 1024, 2688], P('expert', None, 'tensor'), may hold values from -0.1875 to 0.1875
- expert_down: bfloat16 [32, 2688, 1024], P('expert', 'tensor'), may hold values from -0.125 to 0.125
- up_proj: bfloat16 [1024, 4096], P(None, 'tensor'), may hold values from -0.1875 to 0.1875
Outputs:
- layer_out: bfloat16 [16384, 4096], P(('dp', 'expert'), 'tensor'), parts along dimension 0
There are 8 independent parts, one for each index of `dp`. A program takes and returns all parts, laid end to end along the dimension named above; an argument that names none is the same for every part. Nothing has to cross between parts.
Inputs may be any that keep to these rules, and one draw needn't show every extreme that they name: `expert_ids`: each row names 8 different experts; within the rows of one block of 128 tokens no expert is named more than 48 times, a bound that some block reaches.
All inputs are finite; a program needn't handle non-finite values.
Results may differ from a plain program's by a relative error of at most 0.035.
Values may be sent and summed in bfloat16 or wider, within the bound.
No kernel may reach another device: no remote copies, remote signals or barrier semaphores. Data moves between devices by JAX's collectives and lax.ppermute only.
A program may use at most 64 MiB of HBM per device.

v0:
```python
import jax
import jax.numpy as jnp
from jax import lax
from jax.sharding import PartitionSpec as P


def body(
    activations, expert_ids, route_gates, down_proj, expert_gate, expert_up, expert_down, up_proj
):
    tensor_count = lax.axis_size("tensor")
    tensor_pos = lax.axis_index("tensor")
    expert_count = lax.axis_size("expert")
    tok_rows = activations.shape[0]
    top_count = expert_ids.shape[1]
    local_experts = expert_gate.shape[0]
    all_experts = local_experts * expert_count
    latent_width = down_proj.shape[1]
    share_width = latent_width // tensor_count
    capacity = min(tok_rows, tok_rows * top_count * 3 // (2 * all_experts))
    partial_value = jnp.dot(activations, down_proj, preferred_element_type=jnp.float32)
    latent = lax.psum(partial_value.astype(jnp.bfloat16), "tensor")
    share = lax.dynamic_slice_in_dim(latent, tensor_pos * share_width, share_width, 1)
    flat_ids = expert_ids.reshape(-1)
    onehot = (flat_ids[:, None] == jnp.arange(all_experts, dtype=jnp.int32)[None, :]).astype(
        jnp.int32
    )
    before = jnp.cumsum(onehot, axis=0) - onehot
    slot = jnp.sum(before * onehot, axis=1)
    dest = flat_ids * capacity + slot
    route_count = tok_rows * top_count
    owner = (
        jnp.zeros((all_experts * capacity,), jnp.int32)
        .at[dest]
        .set(jnp.arange(route_count, dtype=jnp.int32) + 1)
    )
    filled = owner > 0
    token_idx = jnp.maximum(owner - 1, 0) // top_count
    outgoing = jnp.where(filled[:, None], share[token_idx], jnp.zeros((), jnp.bfloat16))
    outgoing = outgoing.reshape(expert_count, local_experts, capacity, share_width)
    full_rows = lax.all_gather(
        lax.all_to_all(outgoing, "expert", split_axis=0, concat_axis=0, tiled=True),
        "tensor",
        axis=3,
        tiled=True,
    )
    gate = jnp.einsum("seci,eif->secf", full_rows, expert_gate, preferred_element_type=jnp.float32)
    upper = jnp.einsum("seci,eif->secf", full_rows, expert_up, preferred_element_type=jnp.float32)
    hidden = (jax.nn.silu(gate) * upper).astype(jnp.bfloat16)
    terms = jnp.einsum("secf,efi->seci", hidden, expert_down, preferred_element_type=jnp.float32)
    summed = lax.psum_scatter(terms.astype(jnp.bfloat16), "tensor", scatter_dimension=3, tiled=True)
    returned = lax.all_to_all(summed, "expert", split_axis=0, concat_axis=0, tiled=True)
    values = returned.reshape(all_experts * capacity, share_width)[dest]
    values = values.reshape(tok_rows, top_count, share_width).astype(jnp.float32)
    combined = jnp.sum(route_gates[:, :, None] * values, axis=1).astype(jnp.bfloat16)
    result = jnp.dot(
        lax.all_gather(combined, "tensor", axis=1, tiled=True),
        up_proj,
        preferred_element_type=jnp.float32,
    )
    return result.astype(jnp.bfloat16)


def solution(mesh):
    in_specs = (
        P(("dp", "expert"), "tensor"),
        P(("dp", "expert"), None),
        P(("dp", "expert"), None),
        P("tensor", None),
        P("expert", None, "tensor"),
        P("expert", None, "tensor"),
        P("expert", "tensor", None),
        P(None, "tensor"),
    )
    out_specs = P(("dp", "expert"), "tensor")
    return jax.shard_map(body, mesh=mesh, in_specs=in_specs, out_specs=out_specs, check_vma=False)
```

profile of v0, /device:TPU:1, one launch (start us, length us, event | category | flops | bytes accessed | tf_op | source)
XLA Modules:
  0.0 327.3 jit_solution(6658911024027914569)
XLA Ops:
  6.5 0.0 copy-start
  6.5 0.0 all-reduce.2.cloned.1.call-start
  6.5 2.4 convolution_convert_fusion
  8.9 0.0 all-reduce.2.cloned.1.call-update
  9.0 0.0 all-gather.2.cloned.1.call-start
  9.0 0.8 copy.21
  9.8 0.1 eq.29
  9.9 0.1 eq.25
  10.0 0.7 broadcast_multiply_fusion
  10.7 9.0 %reduce-window.6 = s32[32,8,128]{2,1,0:T(8,128)S(1)} reduce-window(s32[32,8,128]{2,1,0:T(8,128)S(1)} %fusion.14, s32[]{:T(128)} %constant.17.clone.1), window={size=1x1x128 pad=0_0x0_0x127_0}, to_apply=%region_0.0 | reduce-window | flops 4161536 | bytes 262148 | tf_op jit(solution)/shard_map/reduce-window
  19.7 0.1 slice.12
  19.8 0.1 copy.23
  20.0 0.1 copy.24
  20.1 0.1 broadcast_add_fusion
  20.2 0.1 copy.20
  20.3 0.1 mul.40
  20.4 4.3 %scatter_custom_fusion = s32[1536]{0:T(1024)S(1)} fusion(s32[1024]{0:T(1024)S(1)} %bitcast.83, s32[1024]{0:T(1024)S(1)} %iota_add_fusion, s32[]{:T(128)} %constant.17.clone.1), kind=kCustom, calls=%fused_computation.38 | custom fusion | bytes 6148 | tf_op jit(solution)/shard_map/scatter | solution.py:34
  24.8 0.1 broadcast_in_dim.22
  24.9 74.8 %all-reduce.2.cloned.1.call-done = bf16[128,1024]{1,0:T(8,128)(2,1)} async-done(((bf16[128,1024]{1,0:T(8,128)(2,1)}), bf16[128,1024]{1,0:T(8,128)(2,1)}) %all-reduce.2.cloned.1.call-update) | async-done | bytes 262160 | tf_op jit(solution)/shard_map/psum | solution.py:21
  99.7 0.8 constant_dynamic-slice_fusion
  100.4 3.2 gather_fusion
  103.6 0.3 broadcast_select_fusion
  103.9 25.7 %all_to_all.10 = bf16[16,2,48,128]{3,2,1,0:T(8,128)(2,1)S(1)} all-to-all(bf16[16,2,48,128]{3,2,1,0:T(8,128)(2,1)S(1)} %broadcast_select_fusion), channel_id=1, replica_groups=mesh['dp'=8,'expert'=16,'tensor'=8] {'expert'}, dimensions={0} | all-to-all | bytes 786432 | tf_op jit(solution)/shard_map/all_to_all | solution.py:41
  129.7 0.8 copy.25
  130.4 0.0 all-gather.2.cloned.1.call-update
  130.5 0.2 reduce-scatter.4.cloned.1.call-start
  130.7 46.3 %all-gather.2.cloned.1.call-done = bf16[16,2,48,1024]{3,2,0,1:T(8,128)(2,1)} async-done(((bf16[16,2,48,128]{3,2,0,1:T(8,128)(2,1)}), bf16[16,2,48,1024]{3,2,0,1:T(8,128)(2,1)}) %all-gather.2.cloned.1.call-update) | async-done | bytes 3145744 | tf_op jit(solution)/shard_map/all_gather | solution.py:40
  177.0 0.0 copy-done.3
  177.0 5.1 %fusion.6 = f32[2,16,48,336]{3,2,1,0:T(8,128)} fusion(bf16[16,2,48,1024]{3,2,0,1:T(8,128)(2,1)} %all-gather.2.cloned.1.call-done, bf16[2,1024,336]{1,2,0:T(8,128)(2,1)S(1)} %copy-done.3), kind=kOutput, calls=%fused_computation.13 | convolution fusion | flops 1056964608 | bytes 6586368 | tf_op jit(solution)/shard_map/seci,eif->secf/dot_general | solution.py:46
  182.2 0.0 copy-done
  182.2 8.2 %convert_bitcast_fusion = bf16[16,2,48,1024]{3,2,0,1:T(8,128)(2,1)} fusion(bf16[2,336,1024]{2,1,0:T(8,128)(2,1)S(1)} %copy-done, f32[2,16,48,336]{3,2,1,0:T(8,128)} %fusion.6, bf16[16,2,48,1024]{3,2,0,1:T(8,128)(2,1)} %all-gather.2.cloned.1.call-done, bf16[2,1024,336]{1,2,0:T(8,128)(2,1)} %param.13), kind=kOutput, calls=%fused_computation.3 | convolution fusion | flops 2118598656 | bytes 11108352 | tf_op jit(solution)/shard_map/secf,efi->seci/dot_general | solution.py:49
  190.4 12.5 %copy.30 = bf16[16,2,48,1024]{2,0,1,3:T(8,128)(2,1)} copy(bf16[16,2,48,1024]{3,2,0,1:T(8,128)(2,1)} %convert_bitcast_fusion) | data formatting | bytes 6291456
  202.9 15.7 %reshape.92 = bf16[1024,1536]{1,0:T(8,128)(2,1)} reshape(bf16[1024,2,16,48]{3,2,1,0:T(8,128)(2,1)} %bitcast.76) | data formatting | bytes 6291456
  218.6 0.0 reduce-scatter.4.cloned.1.call-update
  218.6 0.0 copy-start.2
  218.6 46.9 %reduce-scatter.4.cloned.1.call-done = bf16[128,1536]{1,0:T(8,128)(2,1)} async-done(((bf16[1024,1536]{1,0:T(8,128)(2,1)}), bf16[128,1536]{1,0:T(8,128)(2,1)}) %reduce-scatter.4.cloned.1.call-update) | async-done | bytes 393232
  265.5 2.1 reshape.93
  267.6 0.0 copy-start.1
  267.6 1.8 copy.26
  269.4 10.4 %all-to-all-start.1 = ((bf16[16,2,48,128]{3,2,1,0:T(8,128)(2,1)}), bf16[16,2,48,128]{3,2,1,0:T(8,128)(2,1)S(1)}, u32[]{:S(2)}, u32[]{:S(2)}) async-start(bf16[16,2,48,128]{3,2,1,0:T(8,128)(2,1)} %copy.26), calls=%async_computation.1 | async-start | bytes 786432 | tf_op jit(solution)/shard_map/all_to_all | solution.py:51
  279.8 0.0 copy-done.2
  279.8 0.1 copy.19
  279.9 14.6 %all-to-all-done.1 = bf16[16,2,48,128]{3,2,1,0:T(8,128)(2,1)S(1)} async-done(((bf16[16,2,48,128]{3,2,1,0:T(8,128)(2,1)}), bf16[16,2,48,128]{3,2,1,0:T(8,128)(2,1)S(1)}, u32[]{:S(2)}, u32[]{:S(2)}) %all-to-all-start.1) | async-done | bytes 393248 | tf_op jit(solution)/shard_map/all_to_all | solution.py:51
  294.5 3.2 gather_fusion.1
  297.7 0.2 fusion.10
  297.9 21.9 %all_gather.7 = bf16[128,1024]{1,0:T(8,128)(2,1)S(1)} all-gather(bf16[128,128]{1,0:T(8,128)(2,1)S(1)} %fusion.10), channel_id=1, replica_groups=mesh['dp'=8,'expert'=16,'tensor'=8] {'tensor'}, dimensions={1}, use_global_device_ids=true | all-gather | bytes 294912 | tf_op jit(solution)/shard_map/all_gather | solution.py:56
  319.8 0.0 copy-done.1
  319.8 1.0 convolution_convert_fusion.1
  (11 shorter events, 0.1 us)
Async XLA Ops:
  6.5 175.6 %copy-start = (bf16[2,336,1024]{2,1,0:T(8,128)(2,1)S(1)}, bf16[2,336,1024]{2,1,0:T(8,128)(2,1)}, u32[]{:S(2)}) copy-start(bf16[2,336,1024]{2,1,0:T(8,128)(2,1)} %param.14) | copy-start | bytes 4128772
  6.5 93.1 %all-reduce.2.cloned.1.call-start = ((), (), s32[]{:S(2)}) async-start(), calls=%async_computation.3 | async-start | bytes 524288 | tf_op jit(solution)/shard_map/psum | solution.py:21
  9.0 168.1 %all-gather.2.cloned.1.call-start = ((), (), s32[]{:S(2)}) async-start(), calls=%async_computation.4 | async-start | bytes 3538944 | tf_op jit(solution)/shard_map/all_gather | solution.py:40
  100.4 76.6 %copy-start.3 = (bf16[2,1024,336]{1,2,0:T(8,128)(2,1)S(1)}, bf16[2,1024,336]{1,2,0:T(8,128)(2,1)}, u32[]{:S(2)}) copy-start(bf16[2,1024,336]{1,2,0:T(8,128)(2,1)} %param.12) | copy-start | bytes 4128772
  130.5 135.0 %reduce-scatter.4.cloned.1.call-start = ((), (), s32[]{:S(2)}) async-start(), calls=%async_computation.5 | async-start | bytes 3538944
  218.6 61.1 %copy-start.2 = (f32[128,8]{0,1:T(8,128)S(1)}, f32[128,8]{0,1:T(8,128)}, u32[]{:S(2)}) copy-start(f32[128,8]{0,1:T(8,128)} %param.10) | copy-start | bytes 12292
  267.6 52.2 %copy-start.1 = (bf16[1024,512]{1,0:T(8,128)(2,1)S(1)}, bf16[1024,512]{1,0:T(8,128)(2,1)}, u32[]{:S(2)}) copy-start(bf16[1024,512]{1,0:T(8,128)(2,1)} %param.15) | copy-start | bytes 3145732
  269.4 25.1 %all-to-all-start.1 = ((bf16[16,2,48,128]{3,2,1,0:T(8,128)(2,1)}), bf16[16,2,48,128]{3,2,1,0:T(8,128)(2,1)S(1)}, u32[]{:S(2)}, u32[]{:S(2)}) async-start(bf16[16,2,48,128]{3,2,1,0:T(8,128)(2,1)} %copy.26), calls=%async_computation.1 | async-start | bytes 786432 | tf_op jit(solution)/shard_map/all_to_all | solution.py:51
Sparse Core Ops, SparseCore 0:
  9.7 89.9 all-reduce.1
  130.6 46.4 all-gather.1
  218.8 46.7 reduce-scatter.3
where the time goes:
time: 328 us; the launch traced here: 327 us
  waiting for transfers between devices  183 us (56%)
  blocking collectives  47.6 us (15%)
  local copies, waits for them, and re-layouts  46 us (14%)
  matrix products  16.7 us (5%)
  between operations  13.3 us (4%)
  starting transfers between devices  10.6 us (3%)
  other arithmetic  10.4 us (3%)
    psum x1, waiting for transfers between devices, body(): latent = lax.psum(partial_value.astype(jnp.bfloat16), 'tensor')  74.8 us
    unnamed x4, waiting for transfers between devices  46.9 us
    all_gather x1, waiting for transfers between devices, body(): lax.all_gather(lax.all_to_all(outgoing, 'expert', split_axis=0, concat_ax...  46.3 us
    unnamed x13, local copies, waits for them, and re-layouts  31.2 us
    all_to_all x1, blocking collectives, body(): lax.all_to_all(outgoing, 'expert', split_axis=0, concat_axis=0, tiled=True)  25.7 us
    all_gather x1, blocking collectives, body(): lax.all_gather(combined, 'tensor', axis=1, tiled=True)  21.9 us
    all_to_all x1, waiting for transfers between devices, body(): lax.all_to_all(summed, 'expert', split_axis=0, concat_axis=0, tiled=True)  14.6 us
    all_to_all x1, starting transfers between devices, body(): lax.all_to_all(summed, 'expert', split_axis=0, concat_axis=0, tiled=True)  10.4 us
  transfers between devices with their start and end apart: 4, of which 4 were waited for; matrix products, arithmetic and copies ran while one was open for 5% of the time, Pallas kernels for 0%

commit v1 on v0

v1 whole, which is shorter than its diff:
```python
import jax
import jax.numpy as jnp
from jax import lax
from jax.experimental import pallas as pl
from jax.experimental.pallas import tpu as pltpu
from jax.sharding import Mesh, PartitionSpec as P

F32 = jnp.float32
BF16 = jnp.bfloat16
CAP = 48


def iota(shape, dim):
    return lax.broadcasted_iota(jnp.int32, shape, dim)


def dot(a, b):
    return jnp.dot(a, b, preferred_element_type=F32)


def routes(core, ids_ref, gates_ref, experts, rows):
    ids = ids_ref[...]
    tokens, top = ids.shape
    named = 2 * iota((tokens, experts), 1) + core
    mask = jnp.zeros((tokens, experts), F32)
    gate = jnp.zeros((tokens, experts), F32)
    for k in range(top):
        same = (ids[:, k : k + 1] == named).astype(F32)
        mask += same
        if gates_ref is not None:
            gate += gates_ref[:, k : k + 1] * same
    earlier = (iota((tokens, tokens), 0) > iota((tokens, tokens), 1)).astype(BF16)
    slot = dot(earlier, mask.astype(BF16))
    code = (mask * (slot + 1.0) - 1.0).astype(BF16)
    first = iota((experts, rows), 0) * CAP
    column = iota((experts, rows), 1)
    spread = ((column >= first) & (column < first + CAP)).astype(BF16)
    place = lax.rem(iota((tokens, rows), 1), CAP).astype(F32)
    hit = (dot(code, spread) == place).astype(F32)
    if gates_ref is None:
        return hit.astype(BF16), None, None
    high = gate.astype(BF16)
    low = (gate - high.astype(F32)).astype(BF16)
    return None, (hit * dot(high, spread)).astype(BF16), (hit * dot(low, spread)).astype(BF16)


def dispatch_kernel(core_ref, ids_ref, own_ref, other_ref, out_ref):
    latent = (own_ref[...] + other_ref[...]).astype(BF16)
    hit, _, _ = routes(core_ref[0], ids_ref, None, out_ref.shape[0] // CAP, out_ref.shape[0])
    out_ref[...] = lax.dot_general(
        hit, latent, (((0,), (0,)), ((), ())), preferred_element_type=F32
    ).astype(BF16)


def combine_kernel(core_ref, ids_ref, gates_ref, rows_ref, out_ref):
    rows = rows_ref[...]
    _, high, low = routes(core_ref[0], ids_ref, gates_ref, rows.shape[0] // CAP, rows.shape[0])
    out_ref[...] = dot(high, rows) + dot(low, rows)


def ffn_kernel(core_ref, x_ref, gate_ref, up_ref, down_ref, gate2_ref, up2_ref, down2_ref, out_ref, wide, deep):
    units = gate_ref.shape[2]
    pitch = deep.shape[0] // 2

    @pl.when(pl.program_id(0) == 0)
    def _():
        for i, ref in enumerate((gate_ref, gate2_ref, up_ref, up2_ref)):
            value = ref[0] if len(ref.shape) == 3 else ref[...]
            wide[:, i * pitch : i * pitch + units] = value
            wide[:, i * pitch + units : (i + 1) * pitch] = jnp.zeros((wide.shape[0], pitch - units), BF16)
        for i, ref in enumerate((down_ref, down2_ref)):
            value = ref[0] if len(ref.shape) == 3 else ref[...]
            deep[i * pitch : i * pitch + units, :] = value
            deep[i * pitch + units : (i + 1) * pitch, :] = jnp.zeros((pitch - units, deep.shape[1]), BF16)

    parts, _, width = x_ref.shape
    x = jnp.concatenate([x_ref[i] for i in range(parts)], axis=1)
    both = dot(x, wide[...])
    gate, up = both[:, : 2 * pitch], both[:, 2 * pitch :]
    hidden = (gate / (1.0 + jnp.exp(-gate)) * up).astype(BF16)
    result = dot(hidden, deep[...]).astype(BF16)
    for i in range(parts):
        out_ref[i] = result[:, i * width : (i + 1) * width]


def ffn(core, x, gate, up, down, gate2, up2, down2):
    parts, rows, width = x.shape
    _, latent, units = gate.shape
    pitch = -(-units // 128) * 128
    block = 256
    mine = lambda shape: pl.BlockSpec((1,) + shape, lambda i, c: (c[0], 0, 0))
    whole = lambda shape: pl.BlockSpec(shape, lambda i, c: (0, 0))
    return pl.pallas_call(
        ffn_kernel,
        out_shape=jax.ShapeDtypeStruct((parts, rows, width), BF16),
        grid_spec=pltpu.PrefetchScalarGridSpec(
            num_scalar_prefetch=1,
            grid=(rows // block,),
            in_specs=[
                pl.BlockSpec((parts, block, width), lambda i, c: (0, i, 0)),
                mine((latent, units)),
                mine((latent, units)),
                mine((units, latent)),
                whole((latent, units)),
                whole((latent, units)),
                whole((units, latent)),
            ],
            out_specs=pl.BlockSpec((parts, block, width), lambda i, c: (0, i, 0)),
            scratch_shapes=[pltpu.VMEM((latent, 4 * pitch), BF16), pltpu.VMEM((2 * pitch, latent), BF16)],
        ),
        compiler_params=pltpu.CompilerParams(vmem_limit_bytes=48 << 20),
    )(core, x, gate, up, down, gate2, up2, down2)


def body(activations, expert_ids, route_gates, down_proj, expert_gate, expert_up, expert_down, up_proj):
    chips = lax.axis_size("x")
    owners = lax.axis_size("z")
    core = lax.axis_index("c").astype(jnp.int32)
    tokens = activations.shape[0]
    latent = down_proj.shape[1]
    width = latent // chips
    rows = owners * CAP
    swap = lambda a: lax.ppermute(a, "c", [(0, 1), (1, 0)])
    other = lambda w: swap(lax.dynamic_index_in_dim(w, 1 - core, 0, keepdims=False))
    here = pl.BlockSpec(memory_space=pltpu.VMEM)
    scalar = pl.BlockSpec(memory_space=pltpu.SMEM)
    index = core.reshape(1)

    gate2, up2, down2 = other(expert_gate), other(expert_up), other(expert_down)
    partial = jnp.concatenate(
        [dot(activations, down_proj[:, i * width : (i + 1) * width]).astype(BF16)[None] for i in range(chips)]
    )
    share = jnp.sum(lax.all_to_all(partial, "x", 0, 0, tiled=True).astype(F32), axis=0)
    sent = pl.pallas_call(
        dispatch_kernel,
        out_shape=jax.ShapeDtypeStruct((rows, width), BF16),
        in_specs=[scalar, here, here, here],
        out_specs=here,
    )(index, expert_ids, share, swap(share))
    got = lax.all_to_all(sent.reshape(owners, CAP, width), "z", 0, 0, tiled=True).reshape(rows, width)
    full = lax.all_gather(got, "x", axis=0)
    terms = ffn(index, full, expert_gate, expert_up, expert_down, gate2, up2, down2)
    summed = lax.psum_scatter(terms, "x", scatter_dimension=0, tiled=False)
    back = lax.all_to_all(summed.reshape(owners, CAP, width), "z", 0, 0, tiled=True).reshape(rows, width)
    mine = pl.pallas_call(
        combine_kernel,
        out_shape=jax.ShapeDtypeStruct((tokens, width), F32),
        in_specs=[scalar, here, here, here],
        out_specs=here,
    )(index, expert_ids, route_gates, back)
    combined = (mine + swap(mine)).astype(BF16)
    parts = lax.all_to_all(jnp.broadcast_to(combined[None], (chips, tokens, width)), "x", 0, 0, tiled=True)
    result = sum(dot(parts[i], up_proj[i * width : (i + 1) * width]) for i in range(chips))
    return result.astype(BF16)


def solution(mesh):
    shape = mesh.devices.shape
    split = Mesh(mesh.devices.reshape(shape[0], shape[1], shape[2] // 2, 2), ("dp", "z", "x", "c"))
    tensor = ("x", "c")
    in_specs = (
        P(("dp", "z"), tensor),
        P(("dp", "z"), None),
        P(("dp", "z"), None),
        P(tensor, None),
        P("z", None, tensor),
        P("z", None, tensor),
        P("z", tensor, None),
        P(None, tensor),
    )
    return jax.shard_map(body, mesh=split, in_specs=in_specs, out_specs=P(("dp", "z"), tensor), check_vma=False)
```

time: 328 us -> 210 us (0.64)
  waiting for transfers between devices: 183 us -> 65 us
  starting transfers between devices: 10.6 us -> 51.6 us
  local copies, waits for them, and re-layouts: 46 us -> 14.7 us
  Pallas kernels: 0 us -> 12.8 us
  matrix products: 16.7 us -> 5.96 us
  other arithmetic: 10.4 us -> 0.99 us
  blocking collectives: 47.6 us -> 44.1 us
    psum x1 -> x0, waiting for transfers between devices: 74.8 us -> none  [body(): latent = lax.psum(partial_value.astype(jnp.bfloat16), 'tensor')]
    unnamed x4 -> x2, waiting for transfers between devices: 46.9 us -> 0.03 us
    ppermute x0 -> x5, starting transfers between devices: none -> 38.8 us  [body(): swap = lambda a: lax.ppermute(a, 'c', [(0, 1), (1, 0)])]
    reduce_scatter x0 -> x1, waiting for transfers between devices: none -> 36.4 us  [body(): summed = lax.psum_scatter(terms, 'x', scatter_dimension=0, tiled=False)]
    all_gather x1, waiting for transfers between devices: 46.3 us -> 11.6 us  [body(): full = lax.all_gather(got, 'x', axis=0)]
    unnamed x13 -> x22, local copies, waits for them, and re-layouts: 31.2 us -> 7.92 us
    all_gather x1 -> x0, blocking collectives: 21.9 us -> none  [body(): lax.all_gather(combined, 'tensor', axis=1, tiled=True)]
    all_to_all x1 -> x3, blocking collectives: 25.7 us -> 44.1 us  [the longest x1 24.9 us: body(): lax.all_to_all(sent.reshape(owners, CAP, width), 'z', 0, 0, tiled=True)]
  transfers between devices with their start and end apart: 4 -> 8, of which waited for: 4 -> 5; matrix products, arithmetic and copies ran while one was open for 5% -> 6% of each run, Pallas kernels for 0% -> 0%
where the time goes in v1:
time: 210 us; the launch traced here: 209 us
  waiting for transfers between devices  65 us (31%)
  starting transfers between devices  51.6 us (25%)
  blocking collectives  44.1 us (21%)
  local copies, waits for them, and re-layouts  14.7 us (7%)
  between operations  13.6 us (6%)
  Pallas kernels  12.8 us (6%)
  matrix products  5.96 us (3%)
    ppermute x5, starting transfers between devices, body(): swap = lambda a: lax.ppermute(a, 'c', [(0, 1), (1, 0)])  38.8 us
    reduce_scatter x1, waiting for transfers between devices, body(): summed = lax.psum_scatter(terms, 'x', scatter_dimension=0, tiled=False)  36.4 us
    all_to_all x1, blocking collectives, body(): lax.all_to_all(sent.reshape(owners, CAP, width), 'z', 0, 0, tiled=True)  24.9 us
    all_to_all x1, waiting for transfers between devices, body(): lax.all_to_all(summed.reshape(owners, CAP, width), 'z', 0, 0, tiled=True)  15.5 us
    all_to_all x1, starting transfers between devices, body(): lax.all_to_all(summed.reshape(owners, CAP, width), 'z', 0, 0, tiled=True)  12.7 us
    all_gather x1, waiting for transfers between devices, body(): full = lax.all_gather(got, 'x', axis=0)  11.6 us
    all_to_all x1, blocking collectives, body(): lax.all_to_all(partial, 'x', 0, 0, tiled=True).astype(F32)  10.3 us
    all_to_all x1, blocking collectives, body(): lax.all_to_all(jnp.broadcast_to(combined[None], (chips, tokens, width)),...  8.87 us
  transfers between devices with their start and end apart: 8, of which 5 were waited for; matrix products, arithmetic and copies ran while one was open for 6% of the time, Pallas kernels for 0%

profile of v1, /device:TPU:1, one launch (start us, length us, event | category | flops | bytes accessed | tf_op | source)
XLA Modules:
  0.0 208.8 jit_solution(8423002316237776667)
XLA Ops:
  6.5 0.9 copy-done
  7.4 1.1 fusion.1
  8.6 0.0 copy-start.7
  8.6 1.1 fusion.2
  9.7 1.1 fusion.3
  10.9 1.1 fusion.4
  12.1 0.0 copy-start.2
  12.1 10.3 %all_to_all.20 = bf16[4,128,256]{2,1,0:T(8,128)(2,1)S(1)} all-to-all(bf16[4,128,256]{2,1,0:T(8,128)(2,1)S(1)} %pad_maximum_fusion), channel_id=1, replica_groups=mesh['dp'=8,'z'=16,'x'=4,'c'=2] {'x'}, dimensions={0} | all-to-all | bytes 524288 | tf_op jit(solution)/shard_map/all_to_all | solution.py:133
  22.4 0.0 copy-start.5
  22.4 15.0 %collective-permute-start = (f32[128,256]{1,0:T(8,128)S(1)}, f32[128,256]{1,0:T(8,128)S(1)}, u32[]{:S(2)}, u32[]{:S(2)}) collective-permute-start(f32[128,256]{1,0:T(8,128)S(1)} %convert_reduce_fusion.own_ref), channel_id=1, source_target_pairs={{0,1},{1,0},{2,3},{3,2},{4,5},{5,4},{6,7},{7,6},{8,9},{9,8},{10,11... | collective-permute-start | bytes 393224 | tf_op jit(solution)/shard_map/ppermute | solution.py:123
  37.4 0.7 copy.21.ids_ref
  38.2 0.2 collective-permute-done.other_ref
  38.4 0.6 copy-done.6
  39.0 2.6 %shard_map.82 = bf16[768,256]{1,0:T(8,128)(2,1)} custom-call(s32[1]{0:T(128)} %bitcast.core_ref, s32[128,8]{1,0:T(8,128)} %copy.21.ids_ref, f32[128,256]{1,0:T(8,128)} %copy-done.5, f32[128,256]{1,0:T(8,128)} %copy-done.6), custom_call_target="tpu_custom_call" | custom-call | tf_op jit(solution)/shard_map/pallas_call | solution.py:134
  41.6 24.9 %all_to_all.21 = bf16[16,48,256]{2,1,0:T(8,128)(2,1)} all-to-all(bf16[16,48,256]{2,1,0:T(8,128)(2,1)} %bitcast.37), channel_id=1, replica_groups=mesh['dp'=8,'z'=16,'x'=4,'c'=2] {'z'}, dimensions={0} | all-to-all | bytes 786432 | tf_op jit(solution)/shard_map/all_to_all | solution.py:140
  66.5 0.0 all-gather.2.cloned.1.call-update
  66.6 0.0 reduce-scatter.2.cloned.1.call-start
  66.6 0.0 copy-start.1
  66.6 0.9 dynamic-slice_bitcast_fusion.2
  67.5 9.7 %collective-permute-start.1 = (bf16[1024,336]{0,1:T(8,128)(2,1)}, bf16[1024,336]{0,1:T(8,128)(2,1)}, u32[]{:S(2)}, u32[]{:S(2)}) collective-permute-start(bf16[1024,336]{0,1:T(8,128)(2,1)} %dynamic-slice_bitcast_fusion.2), channel_id=1, source_target_pairs={{0,1},{1,0},{2,3},{3,2},{4,5},{5,4},{6,7},{7,6},{8,9},{9,8},{10,11... | collective-permute-start | bytes 2064392 | tf_op jit(solution)/shard_map/ppermute | solution.py:123
  77.2 2.0 dynamic-slice_bitcast_fusion.1
  79.2 1.9 collective-permute-start.2
  81.2 1.0 dynamic-slice_bitcast_fusion
  82.1 2.4 %collective-permute-start.3 = (bf16[336,1024]{1,0:T(8,128)(2,1)}, bf16[336,1024]{1,0:T(8,128)(2,1)}, u32[]{:S(2)}, u32[]{:S(2)}) collective-permute-start(bf16[336,1024]{1,0:T(8,128)(2,1)} %dynamic-slice_bitcast_fusion), channel_id=1, source_target_pairs={{0,1},{1,0},{2,3},{3,2},{4,5},{5,4},{6,7},{7,6},{8,9},{9,8},{10,11... | collective-permute-start | bytes 2064392 | tf_op jit(solution)/shard_map/ppermute | solution.py:123
  84.5 1.6 copy.17.gate_ref
  86.1 2.6 %copy.18.up_ref = bf16[2,1024,336]{2,1,0:T(8,128)(2,1)} copy(bf16[2,1024,336]{1,2,0:T(8,128)(2,1)} %param.13) | data formatting | bytes 2752512 | tf_op args[5]
  88.7 0.0 collective-permute-done.1
  88.7 1.5 copy.19.gate2_ref
  90.2 0.0 collective-permute-done.2
  90.2 1.5 copy.20.up2_ref
  91.6 11.6 %all-gather.2.cloned.1.call-done.x_ref = bf16[4,768,256]{2,1,0:T(8,128)(2,1)} async-done(((bf16[1,768,256]{2,1,0:T(8,128)(2,1)}), bf16[4,768,256]{2,1,0:T(8,128)(2,1)}) %all-gather.2.cloned.1.call-update) | async-done | bytes 1572880 | tf_op jit(solution)/shard_map/all_gather | solution.py:141
  103.3 7.4 %shard_map.83 = bf16[4,768,256]{2,1,0:T(8,128)(2,1)} custom-call(s32[1]{0:T(128)} %bitcast.core_ref, bf16[4,768,256]{2,1,0:T(8,128)(2,1)} %all-gather.2.cloned.1.call-done.x_ref, bf16[2,1024,336]{2,1,0:T(8,128)(2,1)} %copy.17.gate_ref, bf16[2,1024,336]{2,1,0:T(8,128)(2,1)} %copy.18.up_ref, bf16[2,336,1024]{2,1,0:T(8,128)(2,1)S(1)} %copy-done.1, ...), custom_call_target="tpu_custom_call" | custom-call | tf_op jit(solution)/shard_map/pallas_call | solution.py:93
  110.7 0.0 reduce-scatter.2.cloned.1.call-update
  110.7 0.0 copy-start.4
  110.7 36.4 %reduce-scatter.2.cloned.1.call-done = bf16[1,768,256]{2,1,0:T(8,128)(2,1)} async-done(((bf16[4,768,256]{2,1,0:T(8,128)(2,1)}), bf16[1,768,256]{2,1,0:T(8,128)(2,1)}) %reduce-scatter.2.cloned.1.call-update) | async-done | bytes 393232 | tf_op jit(solution)/shard_map/reduce_scatter | solution.py:143
  147.2 12.7 %all-to-all-start.2 = ((bf16[16,48,256]{2,1,0:T(8,128)(2,1)}), bf16[16,48,256]{2,1,0:T(8,128)(2,1)S(1)}, u32[]{:S(2)}, u32[]{:S(2)}) async-start(bf16[16,48,256]{2,1,0:T(8,128)(2,1)} %bitcast.38), calls=%async_computation.3 | async-start | bytes 786432 | tf_op jit(solution)/shard_map/all_to_all | solution.py:144
  159.9 0.7 copy.22.gates_ref
  160.6 15.5 %all-to-all-done.2 = bf16[16,48,256]{2,1,0:T(8,128)(2,1)S(1)} async-done(((bf16[16,48,256]{2,1,0:T(8,128)(2,1)}), bf16[16,48,256]{2,1,0:T(8,128)(2,1)S(1)}, u32[]{:S(2)}, u32[]{:S(2)}) %all-to-all-start.2) | async-done | bytes 393248 | tf_op jit(solution)/shard_map/all_to_all | solution.py:144
  176.1 0.7 copy-done.3
  176.9 2.7 %shard_map.84 = f32[128,256]{1,0:T(8,128)} custom-call(s32[1]{0:T(128)} %bitcast.core_ref, s32[128,8]{1,0:T(8,128)} %copy.21.ids_ref, f32[128,8]{1,0:T(8,128)} %copy.22.gates_ref, bf16[768,256]{1,0:T(8,128)(2,1)} %bitcast.36), custom_call_target="tpu_custom_call" | custom-call | tf_op jit(solution)/shard_map/pallas_call | solution.py:145
  179.6 9.9 %collective-permute-start.4 = (f32[128,256]{1,0:T(8,128)}, f32[128,256]{1,0:T(8,128)S(1)}, u32[]{:S(2)}, u32[]{:S(2)}) collective-permute-start(f32[128,256]{1,0:T(8,128)} %shard_map.84), channel_id=1, source_target_pairs={{0,1},{1,0},{2,3},{3,2},{4,5},{5,4},{6,7},{7,6},{8,9},{9,8},{10,11... | collective-permute-start | bytes 393224 | tf_op jit(solution)/shard_map/ppermute | solution.py:123
  189.5 1.2 collective-permute-done.4
  190.7 0.9 add_convert_fusion
  191.6 8.9 %all_to_all.22 = bf16[4,128,256]{2,1,0:T(8,128)(2,1)S(1)} all-to-all(bf16[4,128,256]{2,1,0:T(8,128)(2,1)S(1)} %broadcast_in_dim.22), channel_id=1, replica_groups=mesh['dp'=8,'z'=16,'x'=4,'c'=2] {'x'}, dimensions={0} | all-to-all | bytes 524288 | tf_op jit(solution)/shard_map/all_to_all | solution.py:152
  200.5 0.2 fusion.8
  200.7 0.2 convolution_add_fusion.2
  200.9 0.2 convolution_add_fusion.1
  201.1 0.8 fusion
  (15 shorter events, 0.1 us)
Async XLA Ops:
  6.5 0.9 copy-start
  6.5 96.7 %all-gather.2.cloned.1.call-start = ((), (), s32[]{:S(2)}) async-start(), calls=%async_computation.5 | async-start | bytes 1966080 | tf_op jit(solution)/shard_map/all_gather | solution.py:141
  8.6 28.8 %copy-start.7 = (s32[128,8]{0,1:T(8,128)S(1)}, s32[128,8]{0,1:T(8,128)}, u32[]{:S(2)}) copy-start(s32[128,8]{0,1:T(8,128)} %param.9) | copy-start | bytes 12292
  12.1 54.5 %copy-start.2 = (bf16[2,1024,336]{1,2,0:T(8,128)(2,1)S(1)}, bf16[2,1024,336]{1,2,0:T(8,128)(2,1)}, u32[]{:S(2)}) copy-start(bf16[2,1024,336]{1,2,0:T(8,128)(2,1)} %param.12) | copy-start | bytes 4128772
  22.4 15.9 %copy-start.5 = (f32[128,256]{1,0:T(8,128)}, f32[128,256]{1,0:T(8,128)S(1)}, u32[]{:S(2)}) copy-start(f32[128,256]{1,0:T(8,128)S(1)} %convert_reduce_fusion.own_ref) | copy-start | bytes 393220
  22.4 15.9 %collective-permute-start = (f32[128,256]{1,0:T(8,128)S(1)}, f32[128,256]{1,0:T(8,128)S(1)}, u32[]{:S(2)}, u32[]{:S(2)}) collective-permute-start(f32[128,256]{1,0:T(8,128)S(1)} %convert_reduce_fusion.own_ref), channel_id=1, source_target_pairs={{0,1},{1,0},{2,3},{3,2},{4,5},{5,4},{6,7},{7,6},{8,9},{9,8},{10,11... | collective-permute-start | bytes 393224 | tf_op jit(solution)/shard_map/ppermute | solution.py:123
  38.4 0.6 copy-start.6
  66.6 80.6 %reduce-scatter.2.cloned.1.call-start = ((), (), s32[]{:S(2)}) async-start(), calls=%async_computation.6 | async-start | bytes 1966080 | tf_op jit(solution)/shard_map/reduce_scatter | solution.py:143
  66.6 14.5 %copy-start.1 = (bf16[2,336,1024]{2,1,0:T(8,128)(2,1)S(1)}, bf16[2,336,1024]{2,1,0:T(8,128)(2,1)}, u32[]{:S(2)}) copy-start(bf16[2,336,1024]{2,1,0:T(8,128)(2,1)} %down_ref.1) | copy-start | bytes 4128772
  67.5 21.2 %collective-permute-start.1 = (bf16[1024,336]{0,1:T(8,128)(2,1)}, bf16[1024,336]{0,1:T(8,128)(2,1)}, u32[]{:S(2)}, u32[]{:S(2)}) collective-permute-start(bf16[1024,336]{0,1:T(8,128)(2,1)} %dynamic-slice_bitcast_fusion.2), channel_id=1, source_target_pairs={{0,1},{1,0},{2,3},{3,2},{4,5},{5,4},{6,7},{7,6},{8,9},{9,8},{10,11... | collective-permute-start | bytes 2064392 | tf_op jit(solution)/shard_map/ppermute | solution.py:123
  79.2 10.9 %collective-permute-start.2 = (bf16[1024,336]{0,1:T(8,128)(2,1)}, bf16[1024,336]{0,1:T(8,128)(2,1)}, u32[]{:S(2)}, u32[]{:S(2)}) collective-permute-start(bf16[1024,336]{0,1:T(8,128)(2,1)} %dynamic-slice_bitcast_fusion.1), channel_id=1, source_target_pairs={{0,1},{1,0},{2,3},{3,2},{4,5},{5,4},{6,7},{7,6},{8,9},{9,8},{10,11... | collective-permute-start | bytes 2064392 | tf_op jit(solution)/shard_map/ppermute | solution.py:123
  82.1 9.5 %collective-permute-start.3 = (bf16[336,1024]{1,0:T(8,128)(2,1)}, bf16[336,1024]{1,0:T(8,128)(2,1)}, u32[]{:S(2)}, u32[]{:S(2)}) collective-permute-start(bf16[336,1024]{1,0:T(8,128)(2,1)} %dynamic-slice_bitcast_fusion), channel_id=1, source_target_pairs={{0,1},{1,0},{2,3},{3,2},{4,5},{5,4},{6,7},{7,6},{8,9},{9,8},{10,11... | collective-permute-start | bytes 2064392 | tf_op jit(solution)/shard_map/ppermute | solution.py:123
  110.7 49.1 %copy-start.8 = (f32[128,8]{0,1:T(8,128)S(1)}, f32[128,8]{0,1:T(8,128)}, u32[]{:S(2)}) copy-start(f32[128,8]{0,1:T(8,128)} %param.10) | copy-start | bytes 12292
  110.7 89.8 %copy-start.4 = (bf16[1024,512]{1,0:T(8,128)(2,1)S(1)}, bf16[1024,512]{1,0:T(8,128)(2,1)}, u32[]{:S(2)}) copy-start(bf16[1024,512]{1,0:T(8,128)(2,1)} %param.15) | copy-start | bytes 3145732
  147.2 29.0 %all-to-all-start.2 = ((bf16[16,48,256]{2,1,0:T(8,128)(2,1)}), bf16[16,48,256]{2,1,0:T(8,128)(2,1)S(1)}, u32[]{:S(2)}, u32[]{:S(2)}) async-start(bf16[16,48,256]{2,1,0:T(8,128)(2,1)} %bitcast.38), calls=%async_computation.3 | async-start | bytes 786432 | tf_op jit(solution)/shard_map/all_to_all | solution.py:144
  176.1 0.7 copy-start.3
  179.6 11.1 %collective-permute-start.4 = (f32[128,256]{1,0:T(8,128)}, f32[128,256]{1,0:T(8,128)S(1)}, u32[]{:S(2)}, u32[]{:S(2)}) collective-permute-start(f32[128,256]{1,0:T(8,128)} %shard_map.84), channel_id=1, source_target_pairs={{0,1},{1,0},{2,3},{3,2},{4,5},{5,4},{6,7},{7,6},{8,9},{9,8},{10,11... | collective-permute-start | bytes 393224 | tf_op jit(solution)/shard_map/ppermute | solution.py:123
Sparse Core Ops, SparseCore 0:
  66.7 36.5 all-gather.1
  110.9 36.2 reduce-scatter.1

commit v2 on v1

v2 whole, which is shorter than its diff:
```python
import jax
import jax.numpy as jnp
from jax import lax
from jax.experimental import pallas as pl
from jax.experimental.pallas import tpu as pltpu
from jax.sharding import Mesh, PartitionSpec as P

F32 = jnp.float32
BF16 = jnp.bfloat16
CAP = 48


def iota(shape, dim):
    return lax.broadcasted_iota(jnp.int32, shape, dim)


def dot(a, b):
    return jnp.dot(a, b, preferred_element_type=F32)


def dot_dims(a, b, i, j):
    return lax.dot_general(a, b, (((i,), (j,)), ((), ())), preferred_element_type=F32)


def routes_kernel(core_ref, ids_ref, gates_ref, hit_ref, weight_ref):
    ids, gates = ids_ref[...], gates_ref[...]
    top, tokens = ids.shape
    rows = hit_ref.shape[0]
    experts = rows // CAP
    named = 2 * iota((experts, tokens), 0) + core_ref[0]
    mask = jnp.zeros((experts, tokens), F32)
    gate = jnp.zeros((experts, tokens), F32)
    for k in range(top):
        same = (ids[k : k + 1, :] == named).astype(F32)
        mask += same
        gate += gates[k : k + 1, :] * same
    earlier = (iota((tokens, tokens), 0) < iota((tokens, tokens), 1)).astype(BF16)
    slot = dot(mask.astype(BF16), earlier)
    code = (mask * (slot + 1.0) - 1.0).astype(BF16)
    first = iota((rows, experts), 1) * CAP
    row = iota((rows, experts), 0)
    spread = ((row >= first) & (row < first + CAP)).astype(BF16)
    place = lax.rem(iota((rows, tokens), 0), CAP).astype(F32)
    hit = dot(spread, code) == place
    hit_ref[...] = jnp.where(hit, 1.0, 0.0).astype(BF16)
    high = gate.astype(BF16)
    low = (gate - high.astype(F32)).astype(BF16)
    for i, term in enumerate((high, low)):
        weight_ref[i * tokens : (i + 1) * tokens, :] = jnp.where(hit, dot(spread, term), 0.0).T.astype(BF16)


def latent_kernel(a_ref, w_ref, out_ref):
    result = dot(a_ref[...], w_ref[...]).astype(BF16)
    parts, _, width = out_ref.shape
    for i in range(parts):
        first = i // 2 * width
        out_ref[i] = result[:, first : first + width]


def dispatch_kernel(hit_ref, pieces_ref, out_ref):
    latent = sum(pieces_ref[i].astype(F32) for i in range(pieces_ref.shape[0])).astype(BF16)
    out_ref[...] = dot(hit_ref[...], latent).astype(BF16)


def combine_kernel(weight_ref, rows_ref, out_ref):
    both = dot(weight_ref[...], rows_ref[...])
    copies, tokens, _ = out_ref.shape
    result = (both[:tokens] + both[tokens:]).astype(BF16)
    for i in range(copies):
        out_ref[i] = result


def ffn_kernel(x_ref, wide_ref, deep_ref, out_ref):
    parts, _, width = x_ref.shape
    units = deep_ref.shape[0]
    x = jnp.concatenate([x_ref[i] for i in range(parts)], axis=1)
    both = dot_dims(x, wide_ref[...], 1, 1)
    gate, up = both[:, :units], both[:, both.shape[1] - units :]
    hidden = (gate / (1.0 + jnp.exp(-gate)) * up).astype(BF16)
    result = dot(hidden, deep_ref[...]).astype(BF16)
    for i in range(parts):
        out_ref[i] = result[:, i * width : (i + 1) * width]


HERE = pl.BlockSpec(memory_space=pltpu.VMEM)
SCALAR = pl.BlockSpec(memory_space=pltpu.SMEM)


def call(kernel, out, *operands):
    specs = [SCALAR if a.shape == (1,) else HERE for a in operands]
    return pl.pallas_call(kernel, out_shape=out, in_specs=specs, out_specs=jax.tree.map(lambda _: HERE, out))(*operands)


def ffn(x, wide, deep):
    parts, rows, width = x.shape
    block = 256
    spec = pl.BlockSpec((parts, block, width), lambda i: (0, i, 0))
    return pl.pallas_call(
        ffn_kernel,
        out_shape=jax.ShapeDtypeStruct((parts, rows, width), BF16),
        grid=(rows // block,),
        in_specs=[spec, HERE, HERE],
        out_specs=spec,
        compiler_params=pltpu.CompilerParams(vmem_limit_bytes=40 << 20),
    )(x, wide, deep)


def body(activations, expert_ids, route_gates, down_proj, expert_gate, expert_up, expert_down, up_proj):
    chips = lax.axis_size("x")
    owners = lax.axis_size("z")
    core = lax.axis_index("c").astype(jnp.int32)
    index = core.reshape(1)
    tokens = activations.shape[0]
    latent = down_proj.shape[1]
    width = latent // chips
    rows = owners * CAP
    ids, gates = expert_ids.T, route_gates.T
    swap = lambda a: lax.ppermute(a, "c", [(0, 1), (1, 0)])
    pick = lambda w, i: lax.dynamic_index_in_dim(w, i, 0, keepdims=False)
    around = lambda a, axis: lax.all_to_all(a, axis, 0, 0, tiled=True)

    shape = lambda dtype, *sizes: jax.ShapeDtypeStruct(sizes, dtype)
    hit, weight = call(routes_kernel, (shape(BF16, rows, tokens), shape(BF16, 2 * tokens, rows)), index, ids, gates)
    partial = call(latent_kernel, shape(BF16, 2 * chips, tokens, width), activations, down_proj)

    weights = (jnp.swapaxes(expert_gate, 1, 2), jnp.swapaxes(expert_up, 1, 2), expert_down)
    partial, weights = lax.optimization_barrier((partial, weights))
    units = expert_down.shape[1]
    leaving = jnp.concatenate([pick(w, 1 - core) for w in weights])
    pieces = around(partial, ("x", "c"))
    pieces, leaving, hit, weight = lax.optimization_barrier((pieces, leaving, hit, weight))
    got = swap(leaving)
    sent = call(dispatch_kernel, shape(BF16, rows, width), hit, pieces)
    pad = jnp.zeros((-2 * units % 128, latent), BF16)
    gate_own, up_own, down_own = [pick(w, core) for w in weights]
    wide = jnp.concatenate([gate_own, got[:units], pad, up_own, got[units : 2 * units]])
    deep = jnp.concatenate([down_own, got[2 * units :]])

    held = around(sent.reshape(owners, CAP, width), "z").reshape(rows, width)
    held, wide, deep = lax.optimization_barrier((held, wide, deep))
    full = around(jnp.broadcast_to(held[None], (chips, rows, width)), "x")
    terms = around(ffn(full, wide, deep), "x")
    summed = jnp.sum(terms.astype(F32), axis=0).astype(BF16)
    back = around(summed.reshape(owners, CAP, width), "z").reshape(rows, width)
    mine = call(combine_kernel, shape(BF16, 2 * chips, tokens, width), weight, back)
    parts = around(mine, ("x", "c")).reshape(chips, 2, tokens, width)
    parts = (parts[:, 0].astype(F32) + parts[:, 1].astype(F32)).astype(BF16)
    result = sum(dot(parts[i], up_proj[i * width : (i + 1) * width]) for i in range(chips))
    return result.astype(BF16)


def solution(mesh):
    shape = mesh.devices.shape
    split = Mesh(mesh.devices.reshape(shape[0], shape[1], shape[2] // 2, 2), ("dp", "z", "x", "c"))
    tensor = ("x", "c")
    in_specs = (
        P(("dp", "z"), tensor),
        P(("dp", "z"), None),
        P(("dp", "z"), None),
        P(tensor, None),
        P("z", None, tensor),
        P("z", None, tensor),
        P("z", tensor, None),
        P(None, tensor),
    )
    return jax.shard_map(body, mesh=split, in_specs=in_specs, out_specs=P(("dp", "z"), tensor), check_vma=False)
```

time: 210 us -> 163 us (0.78)
  blocking collectives: 44.1 us -> 92.4 us
  waiting for transfers between devices: 65 us -> 19.4 us
  starting transfers between devices: 51.6 us -> 27.1 us
  between operations: 13.6 us -> 0.18 us
  local copies, waits for them, and re-layouts: 14.7 us -> 5.83 us
  matrix products: 5.96 us -> 1.4 us
    all_to_all x3 -> x4, blocking collectives: 44.1 us -> 92.4 us  [body(): around = lambda a, axis: lax.all_to_all(a, axis, 0, 0, tiled=True)]
    reduce_scatter x1 -> x0, waiting for transfers between devices: 36.4 us -> none  [body(): summed = lax.psum_scatter(terms, 'x', scatter_dimension=0, tiled=False)]
    ppermute x5 -> x1, starting transfers between devices: 38.8 us -> 2.77 us  [body(): swap = lambda a: lax.ppermute(a, 'c', [(0, 1), (1, 0)])]
    all_to_all x1 -> x2, starting transfers between devices: 12.7 us -> 24.4 us  [body(): around = lambda a, axis: lax.all_to_all(a, axis, 0, 0, tiled=True)]
    all_gather x1 -> x0, waiting for transfers between devices: 11.6 us -> none  [body(): full = lax.all_gather(got, 'x', axis=0)]
    unnamed x22 -> x16, local copies, waits for them, and re-layouts: 7.92 us -> 3.18 us
    dot_general x8 -> x4, matrix products: 5.96 us -> 1.4 us  [dot(): return jnp.dot(a, b, preferred_element_type=F32)]
    all_to_all x1 -> x2, waiting for transfers between devices: 15.5 us -> 19.4 us  [body(): around = lambda a, axis: lax.all_to_all(a, axis, 0, 0, tiled=True)]
  transfers between devices with their start and end apart: 8 -> 3, of which waited for: 5 -> 2; matrix products, arithmetic and copies ran while one was open for 6% -> 3% of each run, Pallas kernels for 0% -> 3%
where the time goes in v2:
time: 163 us; the launch traced here: 162 us
  blocking collectives  92.4 us (57%)
  starting transfers between devices  27.1 us (17%)
  waiting for transfers between devices  19.4 us (12%)
  Pallas kernels  13.4 us (8%)
  local copies, waits for them, and re-layouts  5.83 us (4%)
  other arithmetic  2.11 us (1%)
    all_to_all x4, blocking collectives, body(): around = lambda a, axis: lax.all_to_all(a, axis, 0, 0, tiled=True)  92.4 us
    all_to_all x2, starting transfers between devices, body(): around = lambda a, axis: lax.all_to_all(a, axis, 0, 0, tiled=True)  24.4 us
    all_to_all x2, waiting for transfers between devices, body(): around = lambda a, axis: lax.all_to_all(a, axis, 0, 0, tiled=True)  19.4 us
    pallas_call x4, Pallas kernels, call(): pl.pallas_call(kernel, out_shape=out, in_specs=specs, out_specs=jax.tree....  8.92 us
    pallas_call x1, Pallas kernels, ffn(): pl.pallas_call(ffn_kernel, out_shape=jax.ShapeDtypeStruct((parts, rows, w...  4.49 us
  transfers between devices with their start and end apart: 3, of which 2 were waited for; matrix products, arithmetic and copies ran while one was open for 3% of the time, Pallas kernels for 3%

profile of v2, /device:TPU:1, one launch (start us, length us, event | category | flops | bytes accessed | tf_op | source)
XLA Modules:
  0.0 161.9 jit_solution(7839345806244398878)
XLA Ops:
  0.0 0.0 copy-start.3
  0.0 2.5 %shard_map.82 = bf16[8,128,256]{2,1,0:T(8,128)(2,1)} custom-call(bf16[128,512]{1,0:T(8,128)(2,1)} %a_ref.1, bf16[512,1024]{1,0:T(8,128)(2,1)} %w_ref.1), custom_call_target="tpu_custom_call" | custom-call | tf_op jit(solution)/shard_map/pallas_call | solution.py:91
  2.5 17.5 %all-to-all-start = ((bf16[8,128,256]{2,1,0:T(8,128)(2,1)}), bf16[8,128,256]{2,1,0:T(8,128)(2,1)S(1)}, u32[]{:S(2)}, u32[]{:S(2)}) async-start(bf16[8,128,256]{2,1,0:T(8,128)(2,1)} %shard_map.82), calls=%async_computation | async-start | bytes 1048576 | tf_op jit(solution)/shard_map/all_to_all | solution.py:120
  20.1 2.0 %shard_map.83 = (bf16[768,128]{1,0:T(8,128)(2,1)}, bf16[256,768]{1,0:T(8,128)(2,1)}) custom-call(s32[1]{0:T(128)} %bitcast.5.core_ref, s32[8,128]{1,0:T(8,128)} %bitcast.43, f32[8,128]{1,0:T(8,128)} %bitcast.44), custom_call_target="tpu_custom_call" | custom-call | tf_op jit(solution)/shard_map/pallas_call | solution.py:91
  22.1 1.1 dynamic-slice_bitcast_fusion.3
  23.2 0.0 copy-done.3
  23.3 1.3 dynamic-slice_bitcast_fusion
  24.6 1.5 pad_maximum_fusion
  26.1 3.5 %all-to-all-done.pieces_ref = bf16[8,128,256]{2,1,0:T(8,128)(2,1)S(1)} async-done(((bf16[8,128,256]{2,1,0:T(8,128)(2,1)}), bf16[8,128,256]{2,1,0:T(8,128)(2,1)S(1)}, u32[]{:S(2)}, u32[]{:S(2)}) %all-to-all-start) | async-done | bytes 524320 | tf_op jit(solution)/shard_map/all_to_all | solution.py:120
  29.6 0.0 copy-start.2
  29.6 2.8 %collective-permute-start = (bf16[1008,1024]{1,0:T(8,128)(2,1)}, bf16[1008,1024]{1,0:T(8,128)(2,1)S(1)}, u32[]{:S(2)}, u32[]{:S(2)}) collective-permute-start(bf16[1008,1024]{1,0:T(8,128)(2,1)} %pad_maximum_fusion), channel_id=1, source_target_pairs={{0,1},{1,0},{2,3},{3,2},{4,5},{5,4},{6,7},{7,6},{8,9},{9,8},{10,11... | collective-permute-start | bytes 6193160 | tf_op jit(solution)/shard_map/ppermute | solution.py:118
  32.4 0.0 copy-done.2
  32.4 2.2 %shard_map.84 = bf16[768,256]{1,0:T(8,128)(2,1)} custom-call(bf16[768,128]{1,0:T(8,128)(2,1)} %get-tuple-element.25.hit_ref, bf16[8,128,256]{2,1,0:T(8,128)(2,1)} %copy-done.2), custom_call_target="tpu_custom_call" | custom-call | tf_op jit(solution)/shard_map/pallas_call | solution.py:91
  34.6 6.8 %all-to-all-start.1 = ((bf16[16,48,256]{2,1,0:T(8,128)(2,1)}), bf16[16,48,256]{2,1,0:T(8,128)(2,1)S(1)}, u32[]{:S(2)}, u32[]{:S(2)}) async-start(bf16[16,48,256]{2,1,0:T(8,128)(2,1)} %bitcast.35), calls=%async_computation.1 | async-start | bytes 786432 | tf_op jit(solution)/shard_map/all_to_all | solution.py:120
  41.4 0.0 copy-start.4
  41.4 1.3 bitcast_dynamic-update-slice_fusion.1
  42.6 0.0 collective-permute-done
  42.7 0.2 copy-done.4
  43.0 0.1 fusion.6
  43.1 0.0 copy-start
  43.1 1.6 copy-done
  44.7 0.1 pad_maximum_fusion.1.deep_ref
  44.8 15.9 %all-to-all-done.1 = bf16[16,48,256]{2,1,0:T(8,128)(2,1)S(1)} async-done(((bf16[16,48,256]{2,1,0:T(8,128)(2,1)}), bf16[16,48,256]{2,1,0:T(8,128)(2,1)S(1)}, u32[]{:S(2)}, u32[]{:S(2)}) %all-to-all-start.1) | async-done | bytes 393248 | tf_op jit(solution)/shard_map/all_to_all | solution.py:120
  60.7 0.1 broadcast_in_dim.10
  60.8 0.0 copy-start.1
  60.8 16.8 %all_to_all.30.x_ref = bf16[4,768,256]{2,1,0:T(8,128)(2,1)S(1)} all-to-all(bf16[4,768,256]{2,1,0:T(8,128)(2,1)S(1)} %broadcast_in_dim.10), channel_id=1, replica_groups=mesh['dp'=8,'z'=16,'x'=4,'c'=2] {'x'}, dimensions={0} | all-to-all | bytes 3145728 | tf_op jit(solution)/shard_map/all_to_all | solution.py:120
  77.6 0.0 copy-done.1
  77.6 4.5 %shard_map.85 = bf16[4,768,256]{2,1,0:T(8,128)(2,1)S(1)} custom-call(bf16[4,768,256]{2,1,0:T(8,128)(2,1)S(1)} %all_to_all.30.x_ref, bf16[1440,1024]{1,0:T(8,128)(2,1)S(1)} %copy-done.1, bf16[672,1024]{1,0:T(8,128)(2,1)S(1)} %pad_maximum_fusion.1.deep_ref), custom_call_target="tpu_custom_call" | custom-call | tf_op jit(solution)/shard_map/pallas_call | solution.py:98
  82.1 15.3 %all_to_all.31 = bf16[4,768,256]{2,1,0:T(8,128)(2,1)S(1)} all-to-all(bf16[4,768,256]{2,1,0:T(8,128)(2,1)S(1)} %shard_map.85), channel_id=1, replica_groups=mesh['dp'=8,'z'=16,'x'=4,'c'=2] {'x'}, dimensions={0} | all-to-all | bytes 3145728 | tf_op jit(solution)/shard_map/all_to_all | solution.py:120
  97.5 0.4 reduce_sum.12
  97.9 0.0 copy-start.5
  97.9 39.4 %all_to_all.32 = bf16[16,48,256]{2,1,0:T(8,128)(2,1)} all-to-all(bf16[16,48,256]{2,1,0:T(8,128)(2,1)S(1)} %bitcast.36), channel_id=1, replica_groups=mesh['dp'=8,'z'=16,'x'=4,'c'=2] {'z'}, dimensions={0} | all-to-all | bytes 786432 | tf_op jit(solution)/shard_map/all_to_all | solution.py:120
  137.4 2.2 %shard_map.86 = bf16[8,128,256]{2,1,0:T(8,128)(2,1)} custom-call(bf16[256,768]{1,0:T(8,128)(2,1)} %get-tuple-element.24.weight_ref, bf16[768,256]{1,0:T(8,128)(2,1)} %bitcast.37), custom_call_target="tpu_custom_call" | custom-call | tf_op jit(solution)/shard_map/pallas_call | solution.py:91
  139.5 20.8 %all_to_all.33 = bf16[8,128,256]{2,1,0:T(8,128)(2,1)S(1)} all-to-all(bf16[8,128,256]{2,1,0:T(8,128)(2,1)} %shard_map.86), channel_id=1, replica_groups=mesh['dp'=8,'z'=16,'x'=4,'c'=2] {'x','c'}, dimensions={0} | all-to-all | bytes 1048576 | tf_op jit(solution)/shard_map/all_to_all | solution.py:120
  160.4 0.1 add_convert_fusion
  160.5 0.0 copy-done.5
  160.5 0.2 fusion.4
  160.7 0.2 convolution_add_fusion.2
  160.9 0.2 convolution_add_fusion.1
  161.0 0.8 fusion
  (3 shorter events, 0.1 us)
Async XLA Ops:
  0.0 23.2 %copy-start.3 = (bf16[2,336,1024]{2,1,0:T(8,128)(2,1)S(1)}, bf16[2,336,1024]{2,1,0:T(8,128)(2,1)}, u32[]{:S(2)}) copy-start(bf16[2,336,1024]{2,1,0:T(8,128)(2,1)} %param.14) | copy-start | bytes 4128772
  2.5 27.0 %all-to-all-start = ((bf16[8,128,256]{2,1,0:T(8,128)(2,1)}), bf16[8,128,256]{2,1,0:T(8,128)(2,1)S(1)}, u32[]{:S(2)}, u32[]{:S(2)}) async-start(bf16[8,128,256]{2,1,0:T(8,128)(2,1)} %shard_map.82), calls=%async_computation | async-start | bytes 1048576 | tf_op jit(solution)/shard_map/all_to_all | solution.py:120
  29.6 2.8 %copy-start.2 = (bf16[8,128,256]{2,1,0:T(8,128)(2,1)}, bf16[8,128,256]{2,1,0:T(8,128)(2,1)S(1)}, u32[]{:S(2)}) copy-start(bf16[8,128,256]{2,1,0:T(8,128)(2,1)S(1)} %all-to-all-done.pieces_ref) | copy-start | bytes 1572868
  29.6 13.1 %collective-permute-start = (bf16[1008,1024]{1,0:T(8,128)(2,1)}, bf16[1008,1024]{1,0:T(8,128)(2,1)S(1)}, u32[]{:S(2)}, u32[]{:S(2)}) collective-permute-start(bf16[1008,1024]{1,0:T(8,128)(2,1)} %pad_maximum_fusion), channel_id=1, source_target_pairs={{0,1},{1,0},{2,3},{3,2},{4,5},{5,4},{6,7},{7,6},{8,9},{9,8},{10,11... | collective-permute-start | bytes 6193160 | tf_op jit(solution)/shard_map/ppermute | solution.py:118
  34.6 26.1 %all-to-all-start.1 = ((bf16[16,48,256]{2,1,0:T(8,128)(2,1)}), bf16[16,48,256]{2,1,0:T(8,128)(2,1)S(1)}, u32[]{:S(2)}, u32[]{:S(2)}) async-start(bf16[16,48,256]{2,1,0:T(8,128)(2,1)} %bitcast.35), calls=%async_computation.1 | async-start | bytes 786432 | tf_op jit(solution)/shard_map/all_to_all | solution.py:120
  41.4 1.5 copy-start.4
  43.1 1.6 copy-start
  60.8 16.8 %copy-start.1 = (bf16[1440,1024]{1,0:T(8,128)(2,1)S(1)}, bf16[1440,1024]{1,0:T(8,128)(2,1)}, u32[]{:S(2)}) copy-start(bf16[1440,1024]{1,0:T(8,128)(2,1)} %copy-done) | copy-start | bytes 8847364
  97.9 62.5 %copy-start.5 = (bf16[1024,512]{1,0:T(8,128)(2,1)S(1)}, bf16[1024,512]{1,0:T(8,128)(2,1)}, u32[]{:S(2)}) copy-start(bf16[1024,512]{1,0:T(8,128)(2,1)} %param.15) | copy-start | bytes 3145732

commit v3 on v2

--- a/solution.py
+++ b/solution.py
@@ -70,39 +70,39 @@
         out_ref[i] = result
 
 
+def output_kernel(own_ref, other_ref, w_ref, out_ref):
+    parts = [(own_ref[i].astype(F32) + other_ref[i].astype(F32)).astype(BF16) for i in range(own_ref.shape[0])]
+    out_ref[...] = dot(jnp.concatenate(parts, axis=1), w_ref[...]).astype(BF16)
+
+
 def ffn_kernel(x_ref, wide_ref, deep_ref, out_ref):
-    parts, _, width = x_ref.shape
+    parts, rows, width = x_ref.shape
     units = deep_ref.shape[0]
-    x = jnp.concatenate([x_ref[i] for i in range(parts)], axis=1)
-    both = dot_dims(x, wide_ref[...], 1, 1)
-    gate, up = both[:, :units], both[:, both.shape[1] - units :]
-    hidden = (gate / (1.0 + jnp.exp(-gate)) * up).astype(BF16)
-    result = dot(hidden, deep_ref[...]).astype(BF16)
-    for i in range(parts):
-        out_ref[i] = result[:, i * width : (i + 1) * width]
+    block = 256
+    for first in range(0, rows, block):
+        here = pl.ds(first, block)
+        x = jnp.concatenate([x_ref[i, here] for i in range(parts)], axis=1)
+        gate = dot_dims(x, wide_ref[:units], 1, 1)
+        up = dot_dims(x, wide_ref[wide_ref.shape[0] - units :], 1, 1)
+        hidden = (gate / (1.0 + jnp.exp(-gate)) * up).astype(BF16)
+        result = dot(hidden, deep_ref[...]).astype(BF16)
+        for i in range(parts):
+            out_ref[i, here] = result[:, i * width : (i + 1) * width]
 
 
 HERE = pl.BlockSpec(memory_space=pltpu.VMEM)
 SCALAR = pl.BlockSpec(memory_space=pltpu.SMEM)
 
 
-def call(kernel, out, *operands):
+def call(kernel, out, *operands, limit=8 << 20):
     specs = [SCALAR if a.shape == (1,) else HERE for a in operands]
-    return pl.pallas_call(kernel, out_shape=out, in_specs=specs, out_specs=jax.tree.map(lambda _: HERE, out))(*operands)
-
-
-def ffn(x, wide, deep):
-    parts, rows, width = x.shape
-    block = 256
-    spec = pl.BlockSpec((parts, block, width), lambda i: (0, i, 0))
     return pl.pallas_call(
-        ffn_kernel,
-        out_shape=jax.ShapeDtypeStruct((parts, rows, width), BF16),
-        grid=(rows // block,),
-        in_specs=[spec, HERE, HERE],
-        out_specs=spec,
-        compiler_params=pltpu.CompilerParams(vmem_limit_bytes=40 << 20),
-    )(x, wide, deep)
+        kernel,
+        out_shape=out,
+        in_specs=specs,
+        out_specs=jax.tree.map(lambda _: HERE, out),
+        compiler_params=pltpu.CompilerParams(vmem_limit_bytes=limit),
+    )(*operands)
 
 
 def body(activations, expert_ids, route_gates, down_proj, expert_gate, expert_up, expert_down, up_proj):
@@ -121,7 +121,7 @@
 
     shape = lambda dtype, *sizes: jax.ShapeDtypeStruct(sizes, dtype)
     hit, weight = call(routes_kernel, (shape(BF16, rows, tokens), shape(BF16, 2 * tokens, rows)), index, ids, gates)
-    partial = call(latent_kernel, shape(BF16, 2 * chips, tokens, width), activations, down_proj)
+    partial = call(latent_kernel, shape(BF16, 2 * chips, tokens, width), activations, down_proj, limit=None)
 
     weights = (jnp.swapaxes(expert_gate, 1, 2), jnp.swapaxes(expert_up, 1, 2), expert_down)
     partial, weights = lax.optimization_barrier((partial, weights))
@@ -139,14 +139,12 @@
     held = around(sent.reshape(owners, CAP, width), "z").reshape(rows, width)
     held, wide, deep = lax.optimization_barrier((held, wide, deep))
     full = around(jnp.broadcast_to(held[None], (chips, rows, width)), "x")
-    terms = around(ffn(full, wide, deep), "x")
+    terms = around(call(ffn_kernel, shape(BF16, chips, rows, width), full, wide, deep, limit=24 << 20), "x")
     summed = jnp.sum(terms.astype(F32), axis=0).astype(BF16)
     back = around(summed.reshape(owners, CAP, width), "z").reshape(rows, width)
-    mine = call(combine_kernel, shape(BF16, 2 * chips, tokens, width), weight, back)
-    parts = around(mine, ("x", "c")).reshape(chips, 2, tokens, width)
-    parts = (parts[:, 0].astype(F32) + parts[:, 1].astype(F32)).astype(BF16)
-    result = sum(dot(parts[i], up_proj[i * width : (i + 1) * width]) for i in range(chips))
-    return result.astype(BF16)
+    mine = call(combine_kernel, shape(BF16, chips, tokens, width), weight, back)
+    parts = around(mine, "x")
+    return call(output_kernel, shape(BF16, tokens, up_proj.shape[1]), parts, swap(parts), up_proj)
 
 
 def solution(mesh):

time: 163 us -> 158 us (0.969)
  blocking collectives: 92.4 us -> 79.2 us
  starting transfers between devices: 27.1 us -> 38.4 us
  Pallas kernels: 13.4 us -> 9.24 us
  local copies, waits for them, and re-layouts: 5.83 us -> 7.95 us
    all_to_all x4, blocking collectives: 92.4 us -> 79.2 us  [body(): around = lambda a, axis: lax.all_to_all(a, axis, 0, 0, tiled=True)]
    ppermute x1 -> x2, starting transfers between devices: 2.77 us -> 13.9 us  [body(): swap = lambda a: lax.ppermute(a, 'c', [(0, 1), (1, 0)])]
    pallas_call x1 -> x0, Pallas kernels: 4.49 us -> none  [ffn(): pl.pallas_call(ffn_kernel, out_shape=jax.ShapeDtypeStruct((parts, rows, w...]
    unnamed x16 -> x18, local copies, waits for them, and re-layouts: 3.18 us -> 3.98 us
    pallas_call x4 -> x6, Pallas kernels: 8.92 us -> 9.24 us  [call(): pl.pallas_call(kernel, out_shape=out, in_specs=specs, out_specs=jax.tree....]
  transfers between devices with their start and end apart: 3 -> 4, of which waited for: 2 -> 3; matrix products, arithmetic and copies ran while one was open for 3% -> 5% of each run, Pallas kernels for 3% -> 1%
where the time goes in v3:
time: 158 us; the launch traced here: 157 us
  blocking collectives  79.2 us (50%)
  starting transfers between devices  38.4 us (24%)
  waiting for transfers between devices  19.9 us (13%)
  Pallas kernels  9.24 us (6%)
  local copies, waits for them, and re-layouts  7.95 us (5%)
  other arithmetic  2.03 us (1%)
    all_to_all x4, blocking collectives, body(): around = lambda a, axis: lax.all_to_all(a, axis, 0, 0, tiled=True)  79.2 us
    all_to_all x2, starting transfers between devices, body(): around = lambda a, axis: lax.all_to_all(a, axis, 0, 0, tiled=True)  24.5 us
    all_to_all x2, waiting for transfers between devices, body(): around = lambda a, axis: lax.all_to_all(a, axis, 0, 0, tiled=True)  18.8 us
    ppermute x2, starting transfers between devices, body(): swap = lambda a: lax.ppermute(a, 'c', [(0, 1), (1, 0)])  13.9 us
    pallas_call x6, Pallas kernels, call(): pl.pallas_call(kernel, out_shape=out, in_specs=specs, out_specs=jax.tree....  9.24 us
    unnamed x18, local copies, waits for them, and re-layouts  3.98 us
  transfers between devices with their start and end apart: 4, of which 3 were waited for; matrix products, arithmetic and copies ran while one was open for 5% of the time, Pallas kernels for 1%

profile of v3, /device:TPU:1, one launch (start us, length us, event | category | flops | bytes accessed | tf_op | source)
XLA Modules:
  0.0 156.9 jit_solution(3594016383960672226)
XLA Ops:
  0.0 0.0 copy-start.5
  0.0 0.0 copy-start.4
  0.0 0.0 copy-start.3
  0.0 2.5 %shard_map.82 = bf16[8,128,256]{2,1,0:T(8,128)(2,1)} custom-call(bf16[128,512]{1,0:T(8,128)(2,1)} %a_ref.1, bf16[512,1024]{1,0:T(8,128)(2,1)} %w_ref.2), custom_call_target="tpu_custom_call" | custom-call | tf_op jit(solution)/shard_map/pallas_call | solution.py:99
  2.5 17.5 %all-to-all-start = ((bf16[8,128,256]{2,1,0:T(8,128)(2,1)}), bf16[8,128,256]{2,1,0:T(8,128)(2,1)S(1)}, u32[]{:S(2)}, u32[]{:S(2)}) async-start(bf16[8,128,256]{2,1,0:T(8,128)(2,1)} %shard_map.82), calls=%async_computation | async-start | bytes 1048576 | tf_op jit(solution)/shard_map/all_to_all | solution.py:120
  20.1 0.0 copy-done.4
  20.1 0.0 copy-done.3
  20.1 0.6 shard_map.83
  20.7 1.2 dynamic-slice_bitcast_fusion.3
  21.8 0.0 copy-done.5
  21.8 1.3 dynamic-slice_bitcast_fusion
  23.1 1.5 pad_maximum_fusion
  24.6 4.9 %all-to-all-done.pieces_ref = bf16[8,128,256]{2,1,0:T(8,128)(2,1)S(1)} async-done(((bf16[8,128,256]{2,1,0:T(8,128)(2,1)}), bf16[8,128,256]{2,1,0:T(8,128)(2,1)S(1)}, u32[]{:S(2)}, u32[]{:S(2)}) %all-to-all-start) | async-done | bytes 524320 | tf_op jit(solution)/shard_map/all_to_all | solution.py:120
  29.6 2.8 %collective-permute-start = (bf16[1008,1024]{1,0:T(8,128)(2,1)}, bf16[1008,1024]{1,0:T(8,128)(2,1)}, u32[]{:S(2)}, u32[]{:S(2)}) collective-permute-start(bf16[1008,1024]{1,0:T(8,128)(2,1)} %pad_maximum_fusion), channel_id=1, source_target_pairs={{0,1},{1,0},{2,3},{3,2},{4,5},{5,4},{6,7},{7,6},{8,9},{9,8},{10,11... | collective-permute-start | bytes 6193160 | tf_op jit(solution)/shard_map/ppermute | solution.py:118
  32.3 1.0 shard_map.84
  33.4 0.0 copy-start.6
  33.4 7.0 %all-to-all-start.1 = ((bf16[16,48,256]{2,1,0:T(8,128)(2,1)}), bf16[16,48,256]{2,1,0:T(8,128)(2,1)S(1)}, u32[]{:S(2)}, u32[]{:S(2)}) async-start(bf16[16,48,256]{2,1,0:T(8,128)(2,1)} %bitcast.8), calls=%async_computation.1 | async-start | bytes 786432 | tf_op jit(solution)/shard_map/all_to_all | solution.py:120
  40.4 1.1 bitcast_dynamic-update-slice_fusion.1
  41.5 0.0 collective-permute-done
  41.5 1.1 slice_dynamic-update-slice_fusion.1
  42.7 0.0 copy-done.6
  42.7 0.1 bitcast_dynamic-update-slice_fusion
  42.8 1.4 fusion
  44.2 0.0 copy-start
  44.2 1.6 %copy-done = bf16[1440,1024]{1,0:T(8,128)(2,1)} copy-done((bf16[1440,1024]{1,0:T(8,128)(2,1)}, bf16[1440,1024]{1,0:T(8,128)(2,1)S(1)}, u32[]{:S(2)}) %copy-start) | copy-done | bytes 2949144
  45.8 0.1 pad_maximum_fusion.1.deep_ref
  45.9 13.8 %all-to-all-done.1 = bf16[16,48,256]{2,1,0:T(8,128)(2,1)S(1)} async-done(((bf16[16,48,256]{2,1,0:T(8,128)(2,1)}), bf16[16,48,256]{2,1,0:T(8,128)(2,1)S(1)}, u32[]{:S(2)}, u32[]{:S(2)}) %all-to-all-start.1) | async-done | bytes 393248 | tf_op jit(solution)/shard_map/all_to_all | solution.py:120
  59.7 0.1 broadcast_in_dim.10
  59.8 0.0 copy-start.1
  59.8 16.8 %all_to_all.30.x_ref = bf16[4,768,256]{2,1,0:T(8,128)(2,1)S(1)} all-to-all(bf16[4,768,256]{2,1,0:T(8,128)(2,1)S(1)} %broadcast_in_dim.10), channel_id=1, replica_groups=mesh['dp'=8,'z'=16,'x'=4,'c'=2] {'x'}, dimensions={0} | all-to-all | bytes 3145728 | tf_op jit(solution)/shard_map/all_to_all | solution.py:120
  76.7 0.0 copy-done.1
  76.7 3.9 %shard_map.85 = bf16[4,768,256]{2,1,0:T(8,128)(2,1)S(1)} custom-call(bf16[4,768,256]{2,1,0:T(8,128)(2,1)S(1)} %all_to_all.30.x_ref, bf16[1440,1024]{1,0:T(8,128)(2,1)S(1)} %copy-done.1, bf16[672,1024]{1,0:T(8,128)(2,1)S(1)} %pad_maximum_fusion.1.deep_ref), custom_call_target="tpu_custom_call" | custom-call | tf_op jit(solution)/shard_map/pallas_call | solution.py:99
  80.5 15.4 %all_to_all.31 = bf16[4,768,256]{2,1,0:T(8,128)(2,1)S(1)} all-to-all(bf16[4,768,256]{2,1,0:T(8,128)(2,1)S(1)} %shard_map.85), channel_id=1, replica_groups=mesh['dp'=8,'z'=16,'x'=4,'c'=2] {'x'}, dimensions={0} | all-to-all | bytes 3145728 | tf_op jit(solution)/shard_map/all_to_all | solution.py:120
  95.9 0.0 copy-start.2
  95.9 0.4 reduce_sum.12
  96.4 39.1 %all_to_all.32 = bf16[16,48,256]{2,1,0:T(8,128)(2,1)S(1)} all-to-all(bf16[16,48,256]{2,1,0:T(8,128)(2,1)S(1)} %bitcast.24), channel_id=1, replica_groups=mesh['dp'=8,'z'=16,'x'=4,'c'=2] {'z'}, dimensions={0} | all-to-all | bytes 786432 | tf_op jit(solution)/shard_map/all_to_all | solution.py:120
  135.5 0.3 shard_map.86
  135.8 7.9 %all_to_all.33.own_ref = bf16[4,128,256]{2,1,0:T(8,128)(2,1)S(1)} all-to-all(bf16[4,128,256]{2,1,0:T(8,128)(2,1)S(1)} %shard_map.86), channel_id=1, replica_groups=mesh['dp'=8,'z'=16,'x'=4,'c'=2] {'x'}, dimensions={0} | all-to-all | bytes 524288 | tf_op jit(solution)/shard_map/all_to_all | solution.py:120
  143.7 11.1 %collective-permute-start.1 = (bf16[4,128,256]{2,1,0:T(8,128)(2,1)S(1)}, bf16[4,128,256]{2,1,0:T(8,128)(2,1)S(1)}, u32[]{:S(2)}, u32[]{:S(2)}) collective-permute-start(bf16[4,128,256]{2,1,0:T(8,128)(2,1)S(1)} %all_to_all.33.own_ref), channel_id=1, source_target_pairs={{0,1},{1,0},{2,3},{3,2},{4,5},{5,4},{6,7},{7,6},{8,9},{9,8},{10,11... | collective-permute-start | bytes 786440 | tf_op jit(solution)/shard_map/ppermute | solution.py:118
  154.8 1.1 collective-permute-done.1.other_ref
  155.9 0.0 copy-done.2
  155.9 1.0 shard_map.87
  (1 shorter events, 0.0 us)
Async XLA Ops:
  0.0 21.8 %copy-start.5 = (bf16[2,336,1024]{2,1,0:T(8,128)(2,1)S(1)}, bf16[2,336,1024]{2,1,0:T(8,128)(2,1)}, u32[]{:S(2)}) copy-start(bf16[2,336,1024]{2,1,0:T(8,128)(2,1)} %param.14) | copy-start | bytes 4128772
  0.0 20.1 %copy-start.4 = (f32[128,8]{0,1:T(8,128)S(1)}, f32[128,8]{0,1:T(8,128)}, u32[]{:S(2)}) copy-start(f32[128,8]{0,1:T(8,128)} %param.10) | copy-start | bytes 12292
  0.0 20.1 %copy-start.3 = (s32[128,8]{0,1:T(8,128)S(1)}, s32[128,8]{0,1:T(8,128)}, u32[]{:S(2)}) copy-start(s32[128,8]{0,1:T(8,128)} %param.9) | copy-start | bytes 12292
  2.5 27.0 %all-to-all-start = ((bf16[8,128,256]{2,1,0:T(8,128)(2,1)}), bf16[8,128,256]{2,1,0:T(8,128)(2,1)S(1)}, u32[]{:S(2)}, u32[]{:S(2)}) async-start(bf16[8,128,256]{2,1,0:T(8,128)(2,1)} %shard_map.82), calls=%async_computation | async-start | bytes 1048576 | tf_op jit(solution)/shard_map/all_to_all | solution.py:120
  29.6 12.0 %collective-permute-start = (bf16[1008,1024]{1,0:T(8,128)(2,1)}, bf16[1008,1024]{1,0:T(8,128)(2,1)}, u32[]{:S(2)}, u32[]{:S(2)}) collective-permute-start(bf16[1008,1024]{1,0:T(8,128)(2,1)} %pad_maximum_fusion), channel_id=1, source_target_pairs={{0,1},{1,0},{2,3},{3,2},{4,5},{5,4},{6,7},{7,6},{8,9},{9,8},{10,11... | collective-permute-start | bytes 6193160 | tf_op jit(solution)/shard_map/ppermute | solution.py:118
  33.4 9.3 %copy-start.6 = (bf16[2,1024,336]{1,2,0:T(8,128)(2,1)S(1)}, bf16[2,1024,336]{1,2,0:T(8,128)(2,1)}, u32[]{:S(2)}) copy-start(bf16[2,1024,336]{1,2,0:T(8,128)(2,1)} %param.13) | copy-start | bytes 4128772
  33.4 26.3 %all-to-all-start.1 = ((bf16[16,48,256]{2,1,0:T(8,128)(2,1)}), bf16[16,48,256]{2,1,0:T(8,128)(2,1)S(1)}, u32[]{:S(2)}, u32[]{:S(2)}) async-start(bf16[16,48,256]{2,1,0:T(8,128)(2,1)} %bitcast.8), calls=%async_computation.1 | async-start | bytes 786432 | tf_op jit(solution)/shard_map/all_to_all | solution.py:120
  44.2 1.6 %copy-start = (bf16[1440,1024]{1,0:T(8,128)(2,1)}, bf16[1440,1024]{1,0:T(8,128)(2,1)S(1)}, u32[]{:S(2)}) copy-start(bf16[1440,1024]{1,0:T(8,128)(2,1)S(1)} %get-tuple-element.29.wide_ref) | copy-start | bytes 8847364
  59.8 16.8 %copy-start.1 = (bf16[1440,1024]{1,0:T(8,128)(2,1)S(1)}, bf16[1440,1024]{1,0:T(8,128)(2,1)}, u32[]{:S(2)}) copy-start(bf16[1440,1024]{1,0:T(8,128)(2,1)} %copy-done) | copy-start | bytes 8847364
  95.9 60.0 %copy-start.2 = (bf16[1024,512]{1,0:T(8,128)(2,1)S(1)}, bf16[1024,512]{1,0:T(8,128)(2,1)}, u32[]{:S(2)}) copy-start(bf16[1024,512]{1,0:T(8,128)(2,1)} %w_ref.3) | copy-start | bytes 3145732
  143.7 12.3 %collective-permute-start.1 = (bf16[4,128,256]{2,1,0:T(8,128)(2,1)S(1)}, bf16[4,128,256]{2,1,0:T(8,128)(2,1)S(1)}, u32[]{:S(2)}, u32[]{:S(2)}) collective-permute-start(bf16[4,128,256]{2,1,0:T(8,128)(2,1)S(1)} %all_to_all.33.own_ref), channel_id=1, source_target_pairs={{0,1},{1,0},{2,3},{3,2},{4,5},{5,4},{6,7},{7,6},{8,9},{9,8},{10,11... | collective-permute-start | bytes 786440 | tf_op jit(solution)/shard_map/ppermute | solution.py:118

commit v4 on v3

--- a/solution.py
+++ b/solution.py
@@ -1,3 +1,5 @@
+import functools
+
 import jax
 import jax.numpy as jnp
 from jax import lax
@@ -75,22 +77,54 @@
     out_ref[...] = dot(jnp.concatenate(parts, axis=1), w_ref[...]).astype(BF16)
 
 
-def ffn_kernel(x_ref, wide_ref, deep_ref, out_ref):
+def assemble_kernel(turn, core_ref, gate_ref, up_ref, down_ref, got_ref, out_ref, held_ref, done):
+    @pl.when(core_ref[0] == turn)
+    def _():
+        units = down_ref.shape[1]
+        loads, stores = [], []
+        for i, ref in enumerate((gate_ref, up_ref, down_ref)):
+            halves = (ref.at[core_ref[0]], got_ref.at[pl.ds(i * units, units)])
+            for j, half in enumerate(halves):
+                n = 2 * i + j
+                place = pl.ds(n * units, units)
+                loads.append(pltpu.make_async_copy(half, held_ref.at[place], done.at[0, n]))
+                stores.append(pltpu.make_async_copy(held_ref.at[place], out_ref.at[place], done.at[1, n]))
+        for load in loads:
+            load.start()
+        for load, store in zip(loads, stores):
+            load.wait()
+            store.start()
+        for store in stores:
+            store.wait()
+
+
+def ffn_kernel(core_ref, x_ref, late_ref, early_ref, out_ref):
     parts, rows, width = x_ref.shape
-    units = deep_ref.shape[0]
     block = 256
-    for first in range(0, rows, block):
-        here = pl.ds(first, block)
-        x = jnp.concatenate([x_ref[i, here] for i in range(parts)], axis=1)
-        gate = dot_dims(x, wide_ref[:units], 1, 1)
-        up = dot_dims(x, wide_ref[wide_ref.shape[0] - units :], 1, 1)
-        hidden = (gate / (1.0 + jnp.exp(-gate)) * up).astype(BF16)
-        result = dot(hidden, deep_ref[...]).astype(BF16)
-        for i in range(parts):
-            out_ref[i, here] = result[:, i * width : (i + 1) * width]
+
+    def run(w_ref):
+        units = w_ref.shape[0] // 3
+        for first in range(0, rows, block):
+            here = pl.ds(first, block)
+            x = jnp.concatenate([x_ref[i, here] for i in range(parts)], axis=1)
+            gate = dot_dims(x, w_ref[:units], 1, 1)
+            up = dot_dims(x, w_ref[units : 2 * units], 1, 1)
+            hidden = (gate / (1.0 + jnp.exp(-gate)) * up).astype(BF16)
+            result = dot(hidden, w_ref[2 * units :]).astype(BF16)
+            for i in range(parts):
+                out_ref[i, here] = result[:, i * width : (i + 1) * width]
+
+    @pl.when(core_ref[0] == 0)
+    def _():
+        run(late_ref)
+
+    @pl.when(core_ref[0] == 1)
+    def _():
+        run(early_ref)
 
 
 HERE = pl.BlockSpec(memory_space=pltpu.VMEM)
+FAR = pl.BlockSpec(memory_space=pl.ANY)
 SCALAR = pl.BlockSpec(memory_space=pltpu.SMEM)
 
 
@@ -131,15 +165,25 @@
     pieces, leaving, hit, weight = lax.optimization_barrier((pieces, leaving, hit, weight))
     got = swap(leaving)
     sent = call(dispatch_kernel, shape(BF16, rows, width), hit, pieces)
-    pad = jnp.zeros((-2 * units % 128, latent), BF16)
-    gate_own, up_own, down_own = [pick(w, core) for w in weights]
-    wide = jnp.concatenate([gate_own, got[:units], pad, up_own, got[units : 2 * units]])
-    deep = jnp.concatenate([down_own, got[2 * units :]])
-
+
+    def assemble(turn, *operands):
+        return pl.pallas_call(
+            functools.partial(assemble_kernel, turn),
+            out_shape=shape(BF16, 6 * units, latent),
+            in_specs=[SCALAR] + [FAR] * 4,
+            out_specs=FAR,
+            scratch_shapes=[pltpu.VMEM((6 * units, latent), BF16), pltpu.SemaphoreType.DMA((2, 6))],
+            compiler_params=pltpu.CompilerParams(vmem_limit_bytes=56 << 20),
+        )(index, *operands)
+
+    whole = assemble(1, *weights, got)
     held = around(sent.reshape(owners, CAP, width), "z").reshape(rows, width)
-    held, wide, deep = lax.optimization_barrier((held, wide, deep))
+    held, whole, weights, got = lax.optimization_barrier((held, whole, weights, got))
+    late = assemble(0, *weights, got)
+    held, whole, late = lax.optimization_barrier((held, whole, late))
     full = around(jnp.broadcast_to(held[None], (chips, rows, width)), "x")
-    terms = around(call(ffn_kernel, shape(BF16, chips, rows, width), full, wide, deep, limit=24 << 20), "x")
+    out = call(ffn_kernel, shape(BF16, chips, rows, width), index, full, late, whole, limit=12 << 20)
+    terms = around(out, "x")
     summed = jnp.sum(terms.astype(F32), axis=0).astype(BF16)
     back = around(summed.reshape(owners, CAP, width), "z").reshape(rows, width)
     mine = call(combine_kernel, shape(BF16, chips, tokens, width), weight, back)

time: 158 us -> 153 us (0.968)
  blocking collectives: 79.2 us -> 71.3 us
  local copies, waits for them, and re-layouts: 7.95 us -> 3.76 us
  Pallas kernels: 9.24 us -> 12.9 us
  waiting for transfers between devices: 19.9 us -> 23 us
    all_to_all x4, blocking collectives: 79.2 us -> 71.3 us  [body(): around = lambda a, axis: lax.all_to_all(a, axis, 0, 0, tiled=True)]
    pallas_call x0 -> x2, Pallas kernels: none -> 3.51 us  [assemble(): pl.pallas_call(functools.partial(assemble_kernel, turn), out_shape=shape(...]
    all_to_all x2, waiting for transfers between devices: 18.8 us -> 21.9 us  [body(): around = lambda a, axis: lax.all_to_all(a, axis, 0, 0, tiled=True)]
    unnamed x18 -> x12, local copies, waits for them, and re-layouts: 3.98 us -> 2.19 us
  transfers between devices with their start and end apart: 4 -> 4, of which waited for: 3 -> 3; matrix products, arithmetic and copies ran while one was open for 5% -> 2% of each run, Pallas kernels for 1% -> 3%
where the time goes in v4:
time: 153 us; the launch traced here: 152 us
  blocking collectives  71.3 us (47%)
  starting transfers between devices  39.4 us (26%)
  waiting for transfers between devices  23 us (15%)
  Pallas kernels  12.9 us (8%)
  local copies, waits for them, and re-layouts  3.76 us (2%)
  other arithmetic  1.94 us (1%)
    all_to_all x4, blocking collectives, body(): around = lambda a, axis: lax.all_to_all(a, axis, 0, 0, tiled=True)  71.3 us
    all_to_all x2, starting transfers between devices, body(): around = lambda a, axis: lax.all_to_all(a, axis, 0, 0, tiled=True)  24.4 us
    all_to_all x2, waiting for transfers between devices, body(): around = lambda a, axis: lax.all_to_all(a, axis, 0, 0, tiled=True)  21.9 us
    ppermute x2, starting transfers between devices, body(): swap = lambda a: lax.ppermute(a, 'c', [(0, 1), (1, 0)])  15 us
    pallas_call x6, Pallas kernels, call(): pl.pallas_call(kernel, out_shape=out, in_specs=specs, out_specs=jax.tree....  9.35 us
    pallas_call x2, Pallas kernels, assemble(): pl.pallas_call(functools.partial(assemble_kernel, turn), out_shape=shape(...  3.51 us
  transfers between devices with their start and end apart: 4, of which 3 were waited for; matrix products, arithmetic and copies ran while one was open for 2% of the time, Pallas kernels for 3%

profile of v4, /device:TPU:1, one launch (start us, length us, event | category | flops | bytes accessed | tf_op | source)
XLA Modules:
  0.0 152.4 jit_solution(390923528828388155)
XLA Ops:
  0.0 0.0 copy-start.5
  0.0 0.0 copy-start.4
  0.0 0.0 copy-start.3
  0.0 2.5 %shard_map.82 = bf16[8,128,256]{2,1,0:T(8,128)(2,1)} custom-call(bf16[128,512]{1,0:T(8,128)(2,1)} %a_ref.1, bf16[512,1024]{1,0:T(8,128)(2,1)} %w_ref.2), custom_call_target="tpu_custom_call" | custom-call | tf_op jit(solution)/shard_map/pallas_call | solution.py:133
  2.5 17.5 %all-to-all-start = ((bf16[8,128,256]{2,1,0:T(8,128)(2,1)}), bf16[8,128,256]{2,1,0:T(8,128)(2,1)S(1)}, u32[]{:S(2)}, u32[]{:S(2)}) async-start(bf16[8,128,256]{2,1,0:T(8,128)(2,1)} %shard_map.82), calls=%async_computation | async-start | bytes 1048576 | tf_op jit(solution)/shard_map/all_to_all | solution.py:154
  20.1 0.0 copy-done.4
  20.1 0.0 copy-done.3
  20.1 0.6 shard_map.83
  20.7 0.0 copy-done.5
  20.7 0.1 dynamic-slice_bitcast_fusion.2
  20.7 1.4 dynamic-slice_bitcast_fusion
  22.2 1.5 pad_maximum_fusion
  23.7 5.9 %all-to-all-done.pieces_ref = bf16[8,128,256]{2,1,0:T(8,128)(2,1)S(1)} async-done(((bf16[8,128,256]{2,1,0:T(8,128)(2,1)}), bf16[8,128,256]{2,1,0:T(8,128)(2,1)S(1)}, u32[]{:S(2)}, u32[]{:S(2)}) %all-to-all-start) | async-done | bytes 524320 | tf_op jit(solution)/shard_map/all_to_all | solution.py:154
  29.6 2.8 %collective-permute-start = (bf16[1008,1024]{1,0:T(8,128)(2,1)}, bf16[1008,1024]{1,0:T(8,128)(2,1)}, u32[]{:S(2)}, u32[]{:S(2)}) collective-permute-start(bf16[1008,1024]{1,0:T(8,128)(2,1)} %pad_maximum_fusion), channel_id=1, source_target_pairs={{0,1},{1,0},{2,3},{3,2},{4,5},{5,4},{6,7},{7,6},{8,9},{9,8},{10,11... | collective-permute-start | bytes 6193160 | tf_op jit(solution)/shard_map/ppermute | solution.py:152
  32.4 1.1 shard_map.84
  33.4 6.8 %all-to-all-start.1 = ((bf16[16,48,256]{2,1,0:T(8,128)(2,1)}), bf16[16,48,256]{2,1,0:T(8,128)(2,1)S(1)}, u32[]{:S(2)}, u32[]{:S(2)}) async-start(bf16[16,48,256]{2,1,0:T(8,128)(2,1)} %bitcast.8), calls=%async_computation.1 | async-start | bytes 786432 | tf_op jit(solution)/shard_map/all_to_all | solution.py:154
  40.2 0.0 collective-permute-done.got_ref
  40.2 3.4 %shard_map.85.early_ref = bf16[2016,1024]{1,0:T(8,128)(2,1)} custom-call(s32[1]{0:T(128)} %bitcast.5.core_ref, bf16[2,336,1024]{2,1,0:T(8,128)(2,1)} %bitcast.18, bf16[2,336,1024]{2,1,0:T(8,128)(2,1)} %bitcast.22, bf16[2,336,1024]{2,1,0:T(8,128)(2,1)} %down_ref.1, bf16[1008,1024]{1,0:T(8,128)(2,1)} %collective-permute-done.got_ref), custom_call_target="tpu_custom_call" | custom-call | tf_op jit(solution)/shard_map/pallas_call | solution.py:170
  43.7 15.9 %all-to-all-done.1 = bf16[16,48,256]{2,1,0:T(8,128)(2,1)S(1)} async-done(((bf16[16,48,256]{2,1,0:T(8,128)(2,1)}), bf16[16,48,256]{2,1,0:T(8,128)(2,1)S(1)}, u32[]{:S(2)}, u32[]{:S(2)}) %all-to-all-start.1) | async-done | bytes 393248 | tf_op jit(solution)/shard_map/all_to_all | solution.py:154
  59.6 0.1 shard_map.86.late_ref
  59.7 0.0 copy-start
  59.7 0.1 broadcast_in_dim.2
  59.8 15.3 %all_to_all.30.x_ref = bf16[4,768,256]{2,1,0:T(8,128)(2,1)S(1)} all-to-all(bf16[4,768,256]{2,1,0:T(8,128)(2,1)S(1)} %broadcast_in_dim.2), channel_id=1, replica_groups=mesh['dp'=8,'z'=16,'x'=4,'c'=2] {'x'}, dimensions={0} | all-to-all | bytes 3145728 | tf_op jit(solution)/shard_map/all_to_all | solution.py:154
  75.1 0.0 copy-done
  75.1 0.0 copy-start.1
  75.1 2.2 %copy-done.1 = bf16[2016,1024]{1,0:T(8,128)(2,1)S(1)} copy-done((bf16[2016,1024]{1,0:T(8,128)(2,1)S(1)}, bf16[2016,1024]{1,0:T(8,128)(2,1)}, u32[]{:S(2)}) %copy-start.1) | copy-done | bytes 4128792
  77.3 4.0 %shard_map.87 = bf16[4,768,256]{2,1,0:T(8,128)(2,1)S(1)} custom-call(s32[1]{0:T(128)} %bitcast.5.core_ref, bf16[4,768,256]{2,1,0:T(8,128)(2,1)S(1)} %all_to_all.30.x_ref, bf16[2016,1024]{1,0:T(8,128)(2,1)S(1)} %copy-done.1, bf16[2016,1024]{1,0:T(8,128)(2,1)S(1)} %copy-done), custom_call_target="tpu_custom_call" | custom-call | tf_op jit(solution)/shard_map/pallas_call | solution.py:133
  81.2 15.0 %all_to_all.31 = bf16[4,768,256]{2,1,0:T(8,128)(2,1)S(1)} all-to-all(bf16[4,768,256]{2,1,0:T(8,128)(2,1)S(1)} %shard_map.87), channel_id=1, replica_groups=mesh['dp'=8,'z'=16,'x'=4,'c'=2] {'x'}, dimensions={0} | all-to-all | bytes 3145728 | tf_op jit(solution)/shard_map/all_to_all | solution.py:154
  96.2 0.0 copy-start.2
  96.2 0.4 reduce_sum.12
  96.7 32.9 %all_to_all.32 = bf16[16,48,256]{2,1,0:T(8,128)(2,1)S(1)} all-to-all(bf16[16,48,256]{2,1,0:T(8,128)(2,1)S(1)} %bitcast.24), channel_id=1, replica_groups=mesh['dp'=8,'z'=16,'x'=4,'c'=2] {'z'}, dimensions={0} | all-to-all | bytes 786432 | tf_op jit(solution)/shard_map/all_to_all | solution.py:154
  129.6 0.3 shard_map.88
  129.8 8.2 %all_to_all.33.own_ref = bf16[4,128,256]{2,1,0:T(8,128)(2,1)S(1)} all-to-all(bf16[4,128,256]{2,1,0:T(8,128)(2,1)S(1)} %shard_map.88), channel_id=1, replica_groups=mesh['dp'=8,'z'=16,'x'=4,'c'=2] {'x'}, dimensions={0} | all-to-all | bytes 524288 | tf_op jit(solution)/shard_map/all_to_all | solution.py:154
  138.1 12.3 %collective-permute-start.1 = (bf16[4,128,256]{2,1,0:T(8,128)(2,1)S(1)}, bf16[4,128,256]{2,1,0:T(8,128)(2,1)S(1)}, u32[]{:S(2)}, u32[]{:S(2)}) collective-permute-start(bf16[4,128,256]{2,1,0:T(8,128)(2,1)S(1)} %all_to_all.33.own_ref), channel_id=1, source_target_pairs={{0,1},{1,0},{2,3},{3,2},{4,5},{5,4},{6,7},{7,6},{8,9},{9,8},{10,11... | collective-permute-start | bytes 786440 | tf_op jit(solution)/shard_map/ppermute | solution.py:152
  150.3 1.1 collective-permute-done.1.other_ref
  151.5 0.0 copy-done.2
  151.5 1.0 shard_map.89
Async XLA Ops:
  0.0 20.7 %copy-start.5 = (bf16[2,1024,336]{1,2,0:T(8,128)(2,1)S(1)}, bf16[2,1024,336]{1,2,0:T(8,128)(2,1)}, u32[]{:S(2)}) copy-start(bf16[2,1024,336]{1,2,0:T(8,128)(2,1)} %param.12) | copy-start | bytes 4128772
  0.0 20.1 %copy-start.4 = (f32[128,8]{0,1:T(8,128)S(1)}, f32[128,8]{0,1:T(8,128)}, u32[]{:S(2)}) copy-start(f32[128,8]{0,1:T(8,128)} %param.10) | copy-start | bytes 12292
  0.0 20.1 %copy-start.3 = (s32[128,8]{0,1:T(8,128)S(1)}, s32[128,8]{0,1:T(8,128)}, u32[]{:S(2)}) copy-start(s32[128,8]{0,1:T(8,128)} %param.9) | copy-start | bytes 12292
  2.5 27.0 %all-to-all-start = ((bf16[8,128,256]{2,1,0:T(8,128)(2,1)}), bf16[8,128,256]{2,1,0:T(8,128)(2,1)S(1)}, u32[]{:S(2)}, u32[]{:S(2)}) async-start(bf16[8,128,256]{2,1,0:T(8,128)(2,1)} %shard_map.82), calls=%async_computation | async-start | bytes 1048576 | tf_op jit(solution)/shard_map/all_to_all | solution.py:154
  29.6 10.7 %collective-permute-start = (bf16[1008,1024]{1,0:T(8,128)(2,1)}, bf16[1008,1024]{1,0:T(8,128)(2,1)}, u32[]{:S(2)}, u32[]{:S(2)}) collective-permute-start(bf16[1008,1024]{1,0:T(8,128)(2,1)} %pad_maximum_fusion), channel_id=1, source_target_pairs={{0,1},{1,0},{2,3},{3,2},{4,5},{5,4},{6,7},{7,6},{8,9},{9,8},{10,11... | collective-permute-start | bytes 6193160 | tf_op jit(solution)/shard_map/ppermute | solution.py:152
  33.4 26.2 %all-to-all-start.1 = ((bf16[16,48,256]{2,1,0:T(8,128)(2,1)}), bf16[16,48,256]{2,1,0:T(8,128)(2,1)S(1)}, u32[]{:S(2)}, u32[]{:S(2)}) async-start(bf16[16,48,256]{2,1,0:T(8,128)(2,1)} %bitcast.8), calls=%async_computation.1 | async-start | bytes 786432 | tf_op jit(solution)/shard_map/all_to_all | solution.py:154
  59.7 15.4 %copy-start = (bf16[2016,1024]{1,0:T(8,128)(2,1)S(1)}, bf16[2016,1024]{1,0:T(8,128)(2,1)}, u32[]{:S(2)}) copy-start(bf16[2016,1024]{1,0:T(8,128)(2,1)} %shard_map.85.early_ref) | copy-start | bytes 12386308
  75.1 2.2 %copy-start.1 = (bf16[2016,1024]{1,0:T(8,128)(2,1)S(1)}, bf16[2016,1024]{1,0:T(8,128)(2,1)}, u32[]{:S(2)}) copy-start(bf16[2016,1024]{1,0:T(8,128)(2,1)} %shard_map.86.late_ref) | copy-start | bytes 12386308
  96.2 55.2 %copy-start.2 = (bf16[1024,512]{1,0:T(8,128)(2,1)S(1)}, bf16[1024,512]{1,0:T(8,128)(2,1)}, u32[]{:S(2)}) copy-start(bf16[1024,512]{1,0:T(8,128)(2,1)} %w_ref.3) | copy-start | bytes 3145732
  138.1 13.4 %collective-permute-start.1 = (bf16[4,128,256]{2,1,0:T(8,128)(2,1)S(1)}, bf16[4,128,256]{2,1,0:T(8,128)(2,1)S(1)}, u32[]{:S(2)}, u32[]{:S(2)}) collective-permute-start(bf16[4,128,256]{2,1,0:T(8,128)(2,1)S(1)} %all_to_all.33.own_ref), channel_id=1, source_target_pairs={{0,1},{1,0},{2,3},{3,2},{4,5},{5,4},{6,7},{7,6},{8,9},{9,8},{10,11... | collective-permute-start | bytes 786440 | tf_op jit(solution)/shard_map/ppermute | solution.py:152

commit v5 on v4

--- a/solution.py
+++ b/solution.py
@@ -66,15 +66,19 @@
 
 def combine_kernel(weight_ref, rows_ref, out_ref):
     both = dot(weight_ref[...], rows_ref[...])
-    copies, tokens, _ = out_ref.shape
-    result = (both[:tokens] + both[tokens:]).astype(BF16)
-    for i in range(copies):
+    tokens = out_ref.shape[0]
+    out_ref[...] = (both[:tokens] + both[tokens:]).astype(BF16)
+
+
+def merge_kernel(own_ref, other_ref, out_ref):
+    result = (own_ref[...].astype(F32) + other_ref[...].astype(F32)).astype(BF16)
+    for i in range(out_ref.shape[0]):
         out_ref[i] = result
 
 
-def output_kernel(own_ref, other_ref, w_ref, out_ref):
-    parts = [(own_ref[i].astype(F32) + other_ref[i].astype(F32)).astype(BF16) for i in range(own_ref.shape[0])]
-    out_ref[...] = dot(jnp.concatenate(parts, axis=1), w_ref[...]).astype(BF16)
+def output_kernel(x_ref, w_ref, out_ref):
+    x = jnp.concatenate([x_ref[i] for i in range(x_ref.shape[0])], axis=1)
+    out_ref[...] = dot(x, w_ref[...]).astype(BF16)
 
 
 def assemble_kernel(turn, core_ref, gate_ref, up_ref, down_ref, got_ref, out_ref, held_ref, done):
@@ -186,9 +190,9 @@
     terms = around(out, "x")
     summed = jnp.sum(terms.astype(F32), axis=0).astype(BF16)
     back = around(summed.reshape(owners, CAP, width), "z").reshape(rows, width)
-    mine = call(combine_kernel, shape(BF16, chips, tokens, width), weight, back)
-    parts = around(mine, "x")
-    return call(output_kernel, shape(BF16, tokens, up_proj.shape[1]), parts, swap(parts), up_proj)
+    mine = call(combine_kernel, shape(BF16, tokens, width), weight, back)
+    both = call(merge_kernel, shape(BF16, chips, tokens, width), mine, swap(mine))
+    return call(output_kernel, shape(BF16, tokens, up_proj.shape[1]), around(both, "x"), up_proj)
 
 
 def solution(mesh):

time: 153 us -> 153 us (level)
    pallas_call x6 -> x7, Pallas kernels: 9.35 us -> 9.36 us  [call(): pl.pallas_call(kernel, out_shape=out, in_specs=specs, out_specs=jax.tree....]
where the time goes in v5:
time: 153 us; the launch traced here: 152 us
  blocking collectives  72 us (47%)
  starting transfers between devices  38.6 us (25%)
  waiting for transfers between devices  22.7 us (15%)
  Pallas kernels  12.9 us (8%)
  local copies, waits for them, and re-layouts  3.76 us (2%)
  other arithmetic  1.94 us (1%)
    all_to_all x4, blocking collectives, body(): around = lambda a, axis: lax.all_to_all(a, axis, 0, 0, tiled=True)  72 us
    all_to_all x2, starting transfers between devices, body(): around = lambda a, axis: lax.all_to_all(a, axis, 0, 0, tiled=True)  24.4 us
    all_to_all x2, waiting for transfers between devices, body(): around = lambda a, axis: lax.all_to_all(a, axis, 0, 0, tiled=True)  21.9 us
    ppermute x2, starting transfers between devices, body(): swap = lambda a: lax.ppermute(a, 'c', [(0, 1), (1, 0)])  14.2 us
    pallas_call x7, Pallas kernels, call(): pl.pallas_call(kernel, out_shape=out, in_specs=specs, out_specs=jax.tree....  9.36 us
    pallas_call x2, Pallas kernels, assemble(): pl.pallas_call(functools.partial(assemble_kernel, turn), out_shape=shape(...  3.51 us
  transfers between devices with their start and end apart: 4, of which 3 were waited for; matrix products, arithmetic and copies ran while one was open for 2% of the time, Pallas kernels for 3%

profile of v5, /device:TPU:1, one launch (start us, length us, event | category | flops | bytes accessed | tf_op | source)
XLA Modules:
  0.0 152.0 jit_solution(12808497846194701093)
XLA Ops:
  0.0 0.0 copy-start.5
  0.0 0.0 copy-start.4
  0.0 0.0 copy-start.3
  0.0 2.5 %shard_map.82 = bf16[8,128,256]{2,1,0:T(8,128)(2,1)} custom-call(bf16[128,512]{1,0:T(8,128)(2,1)} %a_ref.1, bf16[512,1024]{1,0:T(8,128)(2,1)} %w_ref.2), custom_call_target="tpu_custom_call" | custom-call | tf_op jit(solution)/shard_map/pallas_call | solution.py:137
  2.5 17.5 %all-to-all-start = ((bf16[8,128,256]{2,1,0:T(8,128)(2,1)}), bf16[8,128,256]{2,1,0:T(8,128)(2,1)S(1)}, u32[]{:S(2)}, u32[]{:S(2)}) async-start(bf16[8,128,256]{2,1,0:T(8,128)(2,1)} %shard_map.82), calls=%async_computation | async-start | bytes 1048576 | tf_op jit(solution)/shard_map/all_to_all | solution.py:158
  20.1 0.0 copy-done.4
  20.1 0.0 copy-done.3
  20.1 0.6 shard_map.83
  20.7 0.0 copy-done.5
  20.7 0.1 dynamic-slice_bitcast_fusion.2
  20.7 1.4 dynamic-slice_bitcast_fusion
  22.2 1.5 pad_maximum_fusion
  23.7 5.9 %all-to-all-done.pieces_ref = bf16[8,128,256]{2,1,0:T(8,128)(2,1)S(1)} async-done(((bf16[8,128,256]{2,1,0:T(8,128)(2,1)}), bf16[8,128,256]{2,1,0:T(8,128)(2,1)S(1)}, u32[]{:S(2)}, u32[]{:S(2)}) %all-to-all-start) | async-done | bytes 524320 | tf_op jit(solution)/shard_map/all_to_all | solution.py:158
  29.6 2.8 %collective-permute-start = (bf16[1008,1024]{1,0:T(8,128)(2,1)}, bf16[1008,1024]{1,0:T(8,128)(2,1)}, u32[]{:S(2)}, u32[]{:S(2)}) collective-permute-start(bf16[1008,1024]{1,0:T(8,128)(2,1)} %pad_maximum_fusion), channel_id=1, source_target_pairs={{0,1},{1,0},{2,3},{3,2},{4,5},{5,4},{6,7},{7,6},{8,9},{9,8},{10,11... | collective-permute-start | bytes 6193160 | tf_op jit(solution)/shard_map/ppermute | solution.py:156
  32.4 1.1 shard_map.84
  33.4 6.8 %all-to-all-start.1 = ((bf16[16,48,256]{2,1,0:T(8,128)(2,1)}), bf16[16,48,256]{2,1,0:T(8,128)(2,1)S(1)}, u32[]{:S(2)}, u32[]{:S(2)}) async-start(bf16[16,48,256]{2,1,0:T(8,128)(2,1)} %bitcast.8), calls=%async_computation.1 | async-start | bytes 786432 | tf_op jit(solution)/shard_map/all_to_all | solution.py:158
  40.2 0.0 collective-permute-done.got_ref
  40.2 3.4 %shard_map.85.early_ref = bf16[2016,1024]{1,0:T(8,128)(2,1)} custom-call(s32[1]{0:T(128)} %bitcast.5.core_ref, bf16[2,336,1024]{2,1,0:T(8,128)(2,1)} %bitcast.18, bf16[2,336,1024]{2,1,0:T(8,128)(2,1)} %bitcast.22, bf16[2,336,1024]{2,1,0:T(8,128)(2,1)} %down_ref.1, bf16[1008,1024]{1,0:T(8,128)(2,1)} %collective-permute-done.got_ref), custom_call_target="tpu_custom_call" | custom-call | tf_op jit(solution)/shard_map/pallas_call | solution.py:174
  43.7 15.9 %all-to-all-done.1 = bf16[16,48,256]{2,1,0:T(8,128)(2,1)S(1)} async-done(((bf16[16,48,256]{2,1,0:T(8,128)(2,1)}), bf16[16,48,256]{2,1,0:T(8,128)(2,1)S(1)}, u32[]{:S(2)}, u32[]{:S(2)}) %all-to-all-start.1) | async-done | bytes 393248 | tf_op jit(solution)/shard_map/all_to_all | solution.py:158
  59.6 0.1 shard_map.86.late_ref
  59.7 0.0 copy-start
  59.7 0.1 broadcast_in_dim.2
  59.8 15.3 %all_to_all.30.x_ref = bf16[4,768,256]{2,1,0:T(8,128)(2,1)S(1)} all-to-all(bf16[4,768,256]{2,1,0:T(8,128)(2,1)S(1)} %broadcast_in_dim.2), channel_id=1, replica_groups=mesh['dp'=8,'z'=16,'x'=4,'c'=2] {'x'}, dimensions={0} | all-to-all | bytes 3145728 | tf_op jit(solution)/shard_map/all_to_all | solution.py:158
  75.1 0.0 copy-done
  75.1 0.0 copy-start.1
  75.1 2.2 %copy-done.1 = bf16[2016,1024]{1,0:T(8,128)(2,1)S(1)} copy-done((bf16[2016,1024]{1,0:T(8,128)(2,1)S(1)}, bf16[2016,1024]{1,0:T(8,128)(2,1)}, u32[]{:S(2)}) %copy-start.1) | copy-done | bytes 4128792
  77.3 4.0 %shard_map.87 = bf16[4,768,256]{2,1,0:T(8,128)(2,1)S(1)} custom-call(s32[1]{0:T(128)} %bitcast.5.core_ref, bf16[4,768,256]{2,1,0:T(8,128)(2,1)S(1)} %all_to_all.30.x_ref, bf16[2016,1024]{1,0:T(8,128)(2,1)S(1)} %copy-done.1, bf16[2016,1024]{1,0:T(8,128)(2,1)S(1)} %copy-done), custom_call_target="tpu_custom_call" | custom-call | tf_op jit(solution)/shard_map/pallas_call | solution.py:137
  81.2 15.0 %all_to_all.31 = bf16[4,768,256]{2,1,0:T(8,128)(2,1)S(1)} all-to-all(bf16[4,768,256]{2,1,0:T(8,128)(2,1)S(1)} %shard_map.87), channel_id=1, replica_groups=mesh['dp'=8,'z'=16,'x'=4,'c'=2] {'x'}, dimensions={0} | all-to-all | bytes 3145728 | tf_op jit(solution)/shard_map/all_to_all | solution.py:158
  96.2 0.0 copy-start.2
  96.2 0.4 reduce_sum.12
  96.7 32.9 %all_to_all.32 = bf16[16,48,256]{2,1,0:T(8,128)(2,1)S(1)} all-to-all(bf16[16,48,256]{2,1,0:T(8,128)(2,1)S(1)} %bitcast.24), channel_id=1, replica_groups=mesh['dp'=8,'z'=16,'x'=4,'c'=2] {'z'}, dimensions={0} | all-to-all | bytes 786432 | tf_op jit(solution)/shard_map/all_to_all | solution.py:158
  129.6 0.3 shard_map.88.own_ref
  129.8 11.4 %collective-permute-start.1 = (bf16[128,256]{1,0:T(8,128)(2,1)S(1)}, bf16[128,256]{1,0:T(8,128)(2,1)S(1)}, u32[]{:S(2)}, u32[]{:S(2)}) collective-permute-start(bf16[128,256]{1,0:T(8,128)(2,1)S(1)} %shard_map.88.own_ref), channel_id=1, source_target_pairs={{0,1},{1,0},{2,3},{3,2},{4,5},{5,4},{6,7},{7,6},{8,9},{9,8},{10,11... | collective-permute-start | bytes 196616 | tf_op jit(solution)/shard_map/ppermute | solution.py:156
  141.3 0.9 collective-permute-done.1.other_ref
  142.2 8.8 %all_to_all.33.x_ref = bf16[4,128,256]{2,1,0:T(8,128)(2,1)S(1)} all-to-all(bf16[4,128,256]{2,1,0:T(8,128)(2,1)S(1)} %shard_map.89), channel_id=1, replica_groups=mesh['dp'=8,'z'=16,'x'=4,'c'=2] {'x'}, dimensions={0} | all-to-all | bytes 524288 | tf_op jit(solution)/shard_map/all_to_all | solution.py:158
  151.0 0.0 copy-done.2
  151.0 1.0 shard_map.90
  (1 shorter events, 0.0 us)
Async XLA Ops:
  0.0 20.7 %copy-start.5 = (bf16[2,1024,336]{1,2,0:T(8,128)(2,1)S(1)}, bf16[2,1024,336]{1,2,0:T(8,128)(2,1)}, u32[]{:S(2)}) copy-start(bf16[2,1024,336]{1,2,0:T(8,128)(2,1)} %param.12) | copy-start | bytes 4128772
  0.0 20.1 %copy-start.4 = (f32[128,8]{0,1:T(8,128)S(1)}, f32[128,8]{0,1:T(8,128)}, u32[]{:S(2)}) copy-start(f32[128,8]{0,1:T(8,128)} %param.10) | copy-start | bytes 12292
  0.0 20.1 %copy-start.3 = (s32[128,8]{0,1:T(8,128)S(1)}, s32[128,8]{0,1:T(8,128)}, u32[]{:S(2)}) copy-start(s32[128,8]{0,1:T(8,128)} %param.9) | copy-start | bytes 12292
  2.5 27.0 %all-to-all-start = ((bf16[8,128,256]{2,1,0:T(8,128)(2,1)}), bf16[8,128,256]{2,1,0:T(8,128)(2,1)S(1)}, u32[]{:S(2)}, u32[]{:S(2)}) async-start(bf16[8,128,256]{2,1,0:T(8,128)(2,1)} %shard_map.82), calls=%async_computation | async-start | bytes 1048576 | tf_op jit(solution)/shard_map/all_to_all | solution.py:158
  29.6 10.7 %collective-permute-start = (bf16[1008,1024]{1,0:T(8,128)(2,1)}, bf16[1008,1024]{1,0:T(8,128)(2,1)}, u32[]{:S(2)}, u32[]{:S(2)}) collective-permute-start(bf16[1008,1024]{1,0:T(8,128)(2,1)} %pad_maximum_fusion), channel_id=1, source_target_pairs={{0,1},{1,0},{2,3},{3,2},{4,5},{5,4},{6,7},{7,6},{8,9},{9,8},{10,11... | collective-permute-start | bytes 6193160 | tf_op jit(solution)/shard_map/ppermute | solution.py:156
  33.4 26.2 %all-to-all-start.1 = ((bf16[16,48,256]{2,1,0:T(8,128)(2,1)}), bf16[16,48,256]{2,1,0:T(8,128)(2,1)S(1)}, u32[]{:S(2)}, u32[]{:S(2)}) async-start(bf16[16,48,256]{2,1,0:T(8,128)(2,1)} %bitcast.8), calls=%async_computation.1 | async-start | bytes 786432 | tf_op jit(solution)/shard_map/all_to_all | solution.py:158
  59.7 15.4 %copy-start = (bf16[2016,1024]{1,0:T(8,128)(2,1)S(1)}, bf16[2016,1024]{1,0:T(8,128)(2,1)}, u32[]{:S(2)}) copy-start(bf16[2016,1024]{1,0:T(8,128)(2,1)} %shard_map.85.early_ref) | copy-start | bytes 12386308
  75.1 2.2 %copy-start.1 = (bf16[2016,1024]{1,0:T(8,128)(2,1)S(1)}, bf16[2016,1024]{1,0:T(8,128)(2,1)}, u32[]{:S(2)}) copy-start(bf16[2016,1024]{1,0:T(8,128)(2,1)} %shard_map.86.late_ref) | copy-start | bytes 12386308
  96.2 54.8 %copy-start.2 = (bf16[1024,512]{1,0:T(8,128)(2,1)S(1)}, bf16[1024,512]{1,0:T(8,128)(2,1)}, u32[]{:S(2)}) copy-start(bf16[1024,512]{1,0:T(8,128)(2,1)} %w_ref.3) | copy-start | bytes 3145732
  129.8 12.3 %collective-permute-start.1 = (bf16[128,256]{1,0:T(8,128)(2,1)S(1)}, bf16[128,256]{1,0:T(8,128)(2,1)S(1)}, u32[]{:S(2)}, u32[]{:S(2)}) collective-permute-start(bf16[128,256]{1,0:T(8,128)(2,1)S(1)} %shard_map.88.own_ref), channel_id=1, source_target_pairs={{0,1},{1,0},{2,3},{3,2},{4,5},{5,4},{6,7},{7,6},{8,9},{9,8},{10,11... | collective-permute-start | bytes 196616 | tf_op jit(solution)/shard_map/ppermute | solution.py:156
